TPU v7x, 32 devices: a whole 2x2x4 slice. The times are simulated.
32 devices in a mesh: ctx: 16 (over z, y, core), ch: 2 (over x).
Axes of the slice: x: 2, y: 2, z: 4, core: 2. Of those that a mesh axis runs over, the one named last changes fastest.
Arguments:
- tokens: int32 [2048], P('ctx'), may hold values from 0 to 511
- feature_table: bfloat16 [512, 3, 4096], P('ch'), may hold values from -4 to 4
- mr_filter: float32 [128, 256], P(None, 'ch'), may hold values from -4 to 4
- hyena_cot: bfloat16 [2048, 4096], P('ctx', 'ch'), may hold values from -6 to 6
- queries: bfloat16 [2048, 4096], P('ctx', 'ch'), may hold values from -4.5 to 4.5
- keys: bfloat16 [2048, 4096], P('ctx', 'ch'), may hold values from -4.5 to 4.5
- values: bfloat16 [2048, 4096], P('ctx', 'ch'), may hold values from -6 to 6
- attn_cot: bfloat16 [2048, 4096], P('ctx', 'ch'), may hold values from -6 to 6
Outputs:
- hyena_out: bfloat16 [2048, 4096], P('ctx', 'ch')
- feat_grads: bfloat16 [2048, 3, 4096], P('ctx', None, 'ch')
- filter_grad: float32 [128, 256], P(None, 'ch')
- attn_out: bfloat16 [2048, 4096], P('ctx', 'ch')
- queries_grad: bfloat16 [2048, 4096], P('ctx', 'ch')
- keys_grad: bfloat16 [2048, 4096], P('ctx', 'ch')
- values_grad: bfloat16 [2048, 4096], P('ctx', 'ch')
All inputs are finite; a program needn't handle non-finite values.
Results may differ from a plain program's by a relative error of at most 0.018.
Values may be sent and summed in bfloat16 or wider, within the bound.
A program may use at most 128 MiB of HBM per device.

v0:
```python
import jax
import jax.numpy as jnp
from jax import lax
from jax.sharding import PartitionSpec as P

HEAD_DIM = 128


NEG = -1e30


def from_partner(shard, axis, apart):
    return lax.ppermute(shard, axis, [(i, i ^ 1 << apart) for i in range(lax.axis_size(axis))])


def passed_along(value, axis, steps):
    count = lax.axis_size(axis)
    leading, last = (max(0, -steps), min(count, count - steps))
    return lax.ppermute(value, axis, [(source, source + steps) for source in range(leading, last)])


def from_behind(shard, axis, by):
    peers = lax.axis_size(axis)
    return lax.ppermute(shard, axis, [(i, (i + by) % peers) for i in range(peers)])


def depthwise(padded, kernel):
    result = lax.conv_general_dilated(
        padded[None],
        kernel[:, None, :],
        (1,),
        "VALID",
        dimension_numbers=("NWC", "WIO", "NWC"),
        feature_group_count=kernel.shape[1],
        precision=lax.Precision.HIGHEST,
    )
    return result[0]


def heads_in(stacked, position, bit):
    width = stacked.shape[2] // 2
    upper = position // (1 << bit) % 2 == 1
    lower_heads = stacked[:, :, :width]
    upper_heads = stacked[:, :, width:]
    kept = jnp.where(upper, upper_heads, lower_heads)
    given = jnp.where(upper, lower_heads, upper_heads)
    received = from_partner(given, "ctx", bit)
    return jnp.concatenate([jnp.where(upper, received, kept), jnp.where(upper, kept, received)], 1)


def heads_out(stacked, position, bit):
    length = stacked.shape[1] // 2
    upper = position // (1 << bit) % 2 == 1
    lower_rows = stacked[:, :length]
    upper_rows = stacked[:, length:]
    kept = jnp.where(upper, upper_rows, lower_rows)
    given = jnp.where(upper, lower_rows, upper_rows)
    received = from_partner(given, "ctx", bit)
    return jnp.concatenate([jnp.where(upper, received, kept), jnp.where(upper, kept, received)], 2)


def fold_rows(stacked, bits):
    length = stacked.shape[1] // 2
    moving = stacked[:, length:]
    for bit in range(2, bits):
        moving = from_partner(moving, "ctx", bit)
    return jnp.concatenate([stacked[:, :length], moving], 1)


def block_starts(group, length, group_count):
    return (2 * group * length, (2 * group_count - 1 - 2 * group) * length)


def masked_scores(query_block, key_block, query_start, key_start, scale):
    query_pos = query_start + lax.iota(jnp.int32, query_block.shape[0])
    key_pos = key_start + lax.iota(jnp.int32, key_block.shape[0])
    allowed = (key_pos[None, :] <= query_pos[:, None])[None]
    scores = (
        jnp.einsum("qhd,khd->hqk", query_block, key_block, preferred_element_type=jnp.float32)
        * scale
    )
    return (allowed, jnp.where(allowed, scores, NEG))


def keep_state(state):
    return state


def forward_tile(state, query_block, query_start, key_block, value_block, key_start, scale):

    def forward_work(state):
        running_max, running_total, weighted = state
        allowed, scores = masked_scores(query_block, key_block, query_start, key_start, scale)
        new_max = jnp.maximum(running_max, scores.max(axis=-1))
        weights = jnp.where(allowed, jnp.exp(scores - new_max[..., None]), 0.0)
        shrink = jnp.exp(running_max - new_max)
        running_total = running_total * shrink + weights.sum(axis=-1)
        weighted = weighted * shrink[..., None] + jnp.einsum(
            "hqk,khd->hqd",
            weights.astype(jnp.bfloat16),
            value_block,
            preferred_element_type=jnp.float32,
        )
        return (new_max, running_total, weighted)

    return lax.cond(key_start < query_start + query_block.shape[0], forward_work, keep_state, state)


def query_grad_tile(
    query_grad,
    query_block,
    cot_block,
    log_total,
    delta,
    query_start,
    key_block,
    value_block,
    key_start,
    scale,
):

    def query_work(query_grad):
        allowed, scores = masked_scores(query_block, key_block, query_start, key_start, scale)
        probs = jnp.where(allowed, jnp.exp(scores - log_total[..., None]), 0.0)
        dprobs = jnp.einsum(
            "qhd,khd->hqk", cot_block, value_block, preferred_element_type=jnp.float32
        )
        dscores = (probs * (dprobs - delta[..., None])).astype(jnp.bfloat16)
        return (
            query_grad
            + jnp.einsum("hqk,khd->hqd", dscores, key_block, preferred_element_type=jnp.float32)
            * scale
        )

    return lax.cond(
        key_start < query_start + query_block.shape[0], query_work, keep_state, query_grad
    )


def key_grad_tile(
    grads,
    query_block,
    cot_block,
    log_total,
    delta,
    query_start,
    key_block,
    value_block,
    key_start,
    scale,
):

    def key_work(grads):
        key_grad, value_grad = grads
        allowed, scores = masked_scores(query_block, key_block, query_start, key_start, scale)
        probs = jnp.where(allowed, jnp.exp(scores - log_total[..., None]), 0.0)
        value_grad = value_grad + jnp.einsum(
            "hqk,qhd->hkd",
            probs.astype(jnp.bfloat16),
            cot_block,
            preferred_element_type=jnp.float32,
        )
        dprobs = jnp.einsum(
            "qhd,khd->hqk", cot_block, value_block, preferred_element_type=jnp.float32
        )
        dscores = (probs * (dprobs - delta[..., None])).astype(jnp.bfloat16)
        key_grad = (
            key_grad
            + jnp.einsum("hqk,qhd->hkd", dscores, query_block, preferred_element_type=jnp.float32)
            * scale
        )
        return (key_grad, value_grad)

    return lax.cond(key_start < query_start + query_block.shape[0], key_work, keep_state, grads)


def local(tokens, feature_table, mr_filter, hyena_cot, queries, keys, values, attn_cot):
    tok_rows = tokens.shape[0]
    vocab_part = feature_table.shape[0]
    first_id = lax.axis_index("ch") * vocab_part
    matches = tokens[:, None] == first_id + lax.iota(jnp.int32, vocab_part)[None, :]
    partial_rows = jnp.dot(
        matches.astype(jnp.bfloat16),
        feature_table.reshape(vocab_part, -1),
        preferred_element_type=jnp.float32,
    )
    summed = lax.psum_scatter(
        partial_rows.reshape(tok_rows, 3, -1).astype(jnp.bfloat16),
        "ch",
        scatter_dimension=2,
        tiled=True,
    )
    channels = summed.shape[2]
    gate_in = summed[:, 0].astype(jnp.float32)
    gate_out = summed[:, 1].astype(jnp.float32)
    value_in = summed[:, 2].astype(jnp.float32)
    mixed = (gate_in * value_in).astype(jnp.bfloat16)
    taps = mr_filter.shape[0]
    reach = taps - 1
    earlier = passed_along(mixed[tok_rows - reach :], "ctx", 1)
    padded = jnp.concatenate([earlier, mixed], 0).astype(jnp.float32)
    per_channel = jnp.repeat(mr_filter, channels // mr_filter.shape[1], axis=1)
    long_conv, pullback = jax.vjp(depthwise, padded, per_channel[::-1])
    hyena_out = (gate_out * long_conv).astype(jnp.bfloat16)
    cotangent = hyena_cot.astype(jnp.float32)
    conv_cot = (cotangent * gate_out).astype(jnp.bfloat16)
    padded_grad, kernel_grad = pullback(conv_cot.astype(jnp.float32))
    later = passed_along(conv_cot[:reach], "ctx", -1)
    extended = jnp.concatenate([conv_cot, later], 0).astype(jnp.float32)
    mixed_grad = depthwise(extended, per_channel)
    feat_grads = jnp.stack(
        [
            (mixed_grad * value_in).astype(jnp.bfloat16),
            (cotangent * long_conv).astype(jnp.bfloat16),
            (mixed_grad * gate_in).astype(jnp.bfloat16),
        ],
        axis=1,
    )
    local_grad = kernel_grad[::-1].reshape(taps, mr_filter.shape[1], -1).sum(axis=2)
    filter_grad = lax.psum(local_grad, "ctx")
    position = lax.axis_index("ctx")
    stacked = jnp.stack([queries, keys, values, attn_cot])
    for bit in (0, 1):
        stacked = heads_in(stacked, position, bit)
    bits = lax.axis_size("ctx").bit_length() - 1
    stacked = fold_rows(stacked, bits)
    rows = stacked.shape[1]
    length = rows // 2
    heads_here = stacked.shape[2] // HEAD_DIM
    split = stacked.reshape(4, rows, heads_here, HEAD_DIM)
    query_here = split[0]
    key_here = split[1]
    value_here = split[2]
    cot_here = split[3]
    group_count = lax.axis_size("ctx") // 4
    group = position // 4
    mine = block_starts(group, length, group_count)
    scale = HEAD_DIM ** (-0.5)
    query_blocks = (query_here[:length], query_here[length:])
    cot_blocks = (cot_here[:length], cot_here[length:])

    def forward_visit(states, pair, source):
        theirs = block_starts(source, length, group_count)
        updated = []
        for query_side in (0, 1):
            state = states[query_side]
            for key_side in (0, 1):
                state = forward_tile(
                    state,
                    query_blocks[query_side],
                    mine[query_side],
                    pair[0, key_side * length : (key_side + 1) * length],
                    pair[1, key_side * length : (key_side + 1) * length],
                    theirs[key_side],
                    scale,
                )
            updated.append(state)
        return tuple(updated)

    empty = (
        jnp.full((heads_here, length), NEG, jnp.float32),
        jnp.zeros((heads_here, length), jnp.float32),
        jnp.zeros((heads_here, length, HEAD_DIM), jnp.float32),
    )
    pair = jnp.stack([key_here, value_here])
    saved = jnp.zeros((group_count,) + pair.shape, jnp.bfloat16)

    def forward_step(step, carry):
        states, saved, pair = carry
        states = forward_visit(states, pair, (group - step) % group_count)
        saved = lax.dynamic_update_index_in_dim(saved, pair, step, 0)
        pair = from_behind(pair, "ctx", 4)
        return (states, saved, pair)

    states, saved, pair = lax.fori_loop(
        0, group_count - 1, forward_step, ((empty, empty), saved, pair)
    )
    final_step = group_count - 1
    states = forward_visit(states, pair, (group - final_step) % group_count)
    saved = lax.dynamic_update_index_in_dim(saved, pair, final_step, 0)
    out_blocks = []
    log_totals = []
    deltas = []
    for query_side in (0, 1):
        running_max, running_total, weighted = states[query_side]
        output = (weighted / running_total[..., None]).astype(jnp.bfloat16)
        out_blocks.append(output)
        log_totals.append(running_max + jnp.log(running_total))
        cot_heads = jnp.transpose(cot_blocks[query_side], (1, 0, 2)).astype(jnp.float32)
        deltas.append(jnp.sum(cot_heads * output.astype(jnp.float32), axis=-1))
    zero_grad = jnp.zeros((heads_here, length, HEAD_DIM), jnp.float32)

    def query_step(step, grads):
        pair = lax.dynamic_index_in_dim(saved, step, 0, keepdims=False)
        theirs = block_starts((group - step) % group_count, length, group_count)
        updated = []
        for query_side in (0, 1):
            current = grads[query_side]
            for key_side in (0, 1):
                current = query_grad_tile(
                    current,
                    query_blocks[query_side],
                    cot_blocks[query_side],
                    log_totals[query_side],
                    deltas[query_side],
                    mine[query_side],
                    pair[0, key_side * length : (key_side + 1) * length],
                    pair[1, key_side * length : (key_side + 1) * length],
                    theirs[key_side],
                    scale,
                )
            updated.append(current)
        return tuple(updated)

    query_grads = lax.fori_loop(0, group_count, query_step, (zero_grad, zero_grad))

    def key_visit(grads, packed, log_all, delta_all, source):
        theirs = block_starts(source, length, group_count)
        updated = []
        for key_side in (0, 1):
            current = grads[key_side]
            for query_side in (0, 1):
                current = key_grad_tile(
                    current,
                    packed[0, query_side * length : (query_side + 1) * length],
                    packed[1, query_side * length : (query_side + 1) * length],
                    log_all[query_side],
                    delta_all[query_side],
                    theirs[query_side],
                    key_here[key_side * length : (key_side + 1) * length],
                    value_here[key_side * length : (key_side + 1) * length],
                    mine[key_side],
                    scale,
                )
            updated.append(current)
        return tuple(updated)

    def key_step(step, carry):
        grads, packed, log_all, delta_all = carry
        grads = key_visit(grads, packed, log_all, delta_all, (group - step) % group_count)
        packed = from_behind(packed, "ctx", 4)
        log_all, delta_all = from_behind((log_all, delta_all), "ctx", 4)
        return (grads, packed, log_all, delta_all)

    start_grads = ((zero_grad, zero_grad), (zero_grad, zero_grad))
    packed = jnp.stack([query_here, cot_here])
    carry = (start_grads, packed, jnp.stack(log_totals), jnp.stack(deltas))
    grads, packed, log_all, delta_all = lax.fori_loop(0, group_count - 1, key_step, carry)
    grads = key_visit(grads, packed, log_all, delta_all, (group - final_step) % group_count)

    def joined_rows(first_block, second_block):
        whole = jnp.concatenate([first_block, second_block], 1)
        return jnp.transpose(whole, (1, 0, 2)).reshape(rows, -1).astype(jnp.bfloat16)

    result = jnp.stack(
        [
            joined_rows(out_blocks[0], out_blocks[1]),
            joined_rows(query_grads[0], query_grads[1]),
            joined_rows(grads[0][0], grads[1][0]),
            joined_rows(grads[0][1], grads[1][1]),
        ]
    )
    result = fold_rows(result, bits)
    for bit in (1, 0):
        result = heads_out(result, position, bit)
    return (hyena_out, feat_grads, filter_grad, result[0], result[1], result[2], result[3])


def solution(mesh):
    return jax.shard_map(
        local,
        mesh=mesh,
        in_specs=(
            P("ctx"),
            P("ch", None, None),
            P(None, "ch"),
            P("ctx", "ch"),
            P("ctx", "ch"),
            P("ctx", "ch"),
            P("ctx", "ch"),
            P("ctx", "ch"),
        ),
        out_specs=(
            P("ctx", "ch"),
            P("ctx", None, "ch"),
            P(None, "ch"),
            P("ctx", "ch"),
            P("ctx", "ch"),
            P("ctx", "ch"),
            P("ctx", "ch"),
        ),
        check_vma=False,
    )
```

profile of v0, /device:TPU:0, one launch (start us, length us, event | category | flops | bytes accessed | tf_op | source)
XLA Modules:
  0.0 649.7 jit_solution(9035586932145045293)
XLA Ops:
  16.7 23.5 %collective-permute-done.7 = bf16[4,256,512]{2,1,0:T(8,128)(2,1)S(1)} collective-permute-done((bf16[4,256,512]{2,1,0:T(8,128)(2,1)S(1)}, bf16[4,256,512]{2,1,0:T(8,128)(2,1)S(1)}, u32[]{:S(2)}, u32[]{:S(2)}) %collective-permute-start.7) | collective-permute-done | bytes 1048608 | tf_op jit(solution)/shard_map/ppermute | solution.py:13
  42.8 23.0 %collective-permute-done.8 = bf16[4,256,512]{2,1,0:T(8,128)(2,1)} collective-permute-done((bf16[4,256,512]{2,1,0:T(8,128)(2,1)S(1)}, bf16[4,256,512]{2,1,0:T(8,128)(2,1)}, u32[]{:S(2)}, u32[]{:S(2)}) %collective-permute-start.8) | collective-permute-done | bytes 1048608 | tf_op jit(solution)/shard_map/ppermute | solution.py:13
  68.3 8.6 %copy.221 = bf16[256,3,4096]{0,2,1:T(8,128)(2,1)} copy(bf16[256,3,4096]{2,0,1:T(8,128)(2,1)} %param.55) | data formatting | bytes 12582912 | tf_op args[1]
  76.9 6.7 %fusion.210 = bf16[128,3,4096]{2,0,1:T(8,128)(2,1)} fusion(bf16[256,3,4096]{0,2,1:T(8,128)(2,1)} %copy.221, s32[256]{0:T(256)S(1)} %iota_add_fusion.40, s32[128]{0:T(128)S(1)} %copy-done.43), kind=kOutput, calls=%fused_computation.348 | convolution fusion | flops 806912000 | bytes 9438720 | tf_op jit(solution)/shard_map/dot_general | solution.py:182
  87.1 26.1 %collective-permute-done.9 = bf16[4,256,512]{2,1,0:T(8,128)(2,1)S(1)} collective-permute-done((bf16[4,256,512]{2,1,0:T(8,128)(2,1)}, bf16[4,256,512]{2,1,0:T(8,128)(2,1)S(1)}, u32[]{:S(2)}, u32[]{:S(2)}) %collective-permute-start.9) | collective-permute-done | bytes 1048608 | tf_op jit(solution)/shard_map/ppermute | solution.py:13
  120.4 76.8 %while.79 = (s32[]{:T(128)}, f32[4,256]{1,0:T(4,128)S(1)}, f32[4,256]{1,0:T(4,128)S(1)}, f32[4,256,128]{2,1,0:T(8,128)S(1)}, f32[4,256]{1,0:T(4,128)S(1)}, /*ind...) while((s32[]{:T(128)}, f32[4,256]{1,0:T(4,128)S(1)}, ...), condition=%wide.region_20.21_spmd, body=%wide.region_3.20_spmd.sunk | while | flops 547629056 | bytes 33833968 | solution.py:275
  129.7 17.2 %collective-permute-done = bf16[2,512,4,128]{3,1,2,0:T(8,128)(2,1)S(1)} collective-permute-done((bf16[2,512,4,128]{3,1,2,0:T(8,128)(2,1)S(1)}, bf16[2,512,4,128]{3,1,2,0:T(8,128)(2,1)S(1)}, u32[]{:S(2)}, u32[]{:S(2)}) %collective-permute-start) | collective-permute-done | bytes 1048608 | tf_op jit(solution)/shard_map/while/body/eval_jaxpr/ppermute | solution.py:24
  153.6 18.9 %collective-permute-done = bf16[2,512,4,128]{3,1,2,0:T(8,128)(2,1)S(1)} collective-permute-done((bf16[2,512,4,128]{3,1,2,0:T(8,128)(2,1)S(1)}, bf16[2,512,4,128]{3,1,2,0:T(8,128)(2,1)S(1)}, u32[]{:S(2)}, u32[]{:S(2)}) %collective-permute-start) | collective-permute-done | bytes 1048608 | tf_op jit(solution)/shard_map/while/body/eval_jaxpr/ppermute | solution.py:24
  179.2 17.9 %collective-permute-done = bf16[2,512,4,128]{3,1,2,0:T(8,128)(2,1)S(1)} collective-permute-done((bf16[2,512,4,128]{3,1,2,0:T(8,128)(2,1)S(1)}, bf16[2,512,4,128]{3,1,2,0:T(8,128)(2,1)S(1)}, u32[]{:S(2)}, u32[]{:S(2)}) %collective-permute-start) | collective-permute-done | bytes 1048608 | tf_op jit(solution)/shard_map/while/body/eval_jaxpr/ppermute | solution.py:24
  215.6 73.1 %while.81 = (s32[]{:T(128)}, f32[4,256,128]{2,1,0:T(8,128)S(1)}, f32[4,256,128]{2,1,0:T(8,128)}, f32[4,256,128]{2,1,0:T(8,128)}, f32[4,256,128]{2,1,0:T(8,128)},...) while((s32[]{:T(128)}, f32[4,256,128]{2,1,0:T(8,128)S(1)}, ...), condition=%wide.region_58.59_spmd, body=%wide.region_49.0_spmd.sunk | while | flops 1083967488 | bytes 43697244 | solution.py:348
  220.7 6.2 conditional.51
  226.9 5.4 conditional.48
  257.6 7.5 %collective-permute-done.2 = f32[2,4,256]{2,1,0:T(4,128)S(1)} collective-permute-done((f32[2,4,256]{2,1,0:T(4,128)S(1)}, f32[2,4,256]{2,1,0:T(4,128)S(1)}, u32[]{:S(2)}, u32[]{:S(2)}) %collective-permute-start.2) | collective-permute-done | bytes 8224 | tf_op jit(solution)/shard_map/while/body/eval_jaxpr/ppermute | solution.py:24
  270.7 5.4 conditional.48
  281.2 7.5 %collective-permute-done.2 = f32[2,4,256]{2,1,0:T(4,128)S(1)} collective-permute-done((f32[2,4,256]{2,1,0:T(4,128)S(1)}, f32[2,4,256]{2,1,0:T(4,128)S(1)}, u32[]{:S(2)}, u32[]{:S(2)}) %collective-permute-start.2) | collective-permute-done | bytes 8224 | tf_op jit(solution)/shard_map/while/body/eval_jaxpr/ppermute | solution.py:24
  290.2 13.3 %conditional.24 = ((f32[4,256,128]{2,1,0:T(8,128)S(1)}, f32[4,256,128]{2,1,0:T(8,128)S(1)})) conditional(s32[]{:T(128)} %convert_element_type.371, (f32[4,256,128]{2,1,0:T(8,128)S(1)}, f32[4,256,128]{2,1,0:T(8,128)S(1)}) %tuple.570, (s32[]{:T(128)}, s32[]{:T(128)}, bf16[256,4,128]{2,0,1:T(8,128)(2,1)S(1)}, bf16[256,4,128]{2,1,0:T(4,128)(2,1)}, ...), branch_computations={%region_59.60_spmd, %region_60.61_spmd} | conditional | flops 270991872 | bytes 6959136 | solution.py:174
  314.6 41.3 %while.80 = (s32[]{:T(128)}, f32[4,256,128]{2,1,0:T(8,128)S(1)}, f32[4,256,128]{2,1,0:T(8,128)S(1)}, s32[]{:T(128)}, s32[]{:T(128)}, /*index=5*/bf16[4,2,512,4,1...) while((s32[]{:T(128)}, f32[4,256,128]{2,1,0:T(8,128)S(1)}, ...), condition=%wide.region_48.49_spmd, body=%wide.region_39.48_spmd.sunk | while | flops 813959168 | bytes 22594336 | solution.py:315
  367.2 17.2 %collective-permute-done.10 = bf16[4,256,512]{2,1,0:T(8,128)(2,1)} collective-permute-done((bf16[4,256,512]{2,1,0:T(8,128)(2,1)}, bf16[4,256,512]{2,1,0:T(8,128)(2,1)}, u32[]{:S(2)}, u32[]{:S(2)}) %collective-permute-start.10) | collective-permute-done | bytes 1048608 | tf_op jit(solution)/shard_map/ppermute | solution.py:13
  389.1 11.4 %fusion.213 = f32[1,128,2048]{2,0,1:T(1,128)S(1)} fusion(f32[128,1,2048]{2,1,0:T(1,128)S(1)} %copy-done.34, bf16[1,255,2048]{2,1,0:T(8,128)(2,1)S(1)} %maximum_bitcast_fusion.1), kind=kOutput, calls=%fused_computation.366 | convolution fusion | flops 402653184 | bytes 3141632 | tf_op jit(solution)/shard_map/conv_general_dilated | solution.py:28
  405.9 5.8 rev.6
  415.9 7.7 %collective-permute-done.11 = bf16[4,256,512]{2,1,0:T(8,128)(2,1)} collective-permute-done((bf16[4,256,512]{2,1,0:T(8,128)(2,1)}, bf16[4,256,512]{2,1,0:T(8,128)(2,1)}, u32[]{:S(2)}, u32[]{:S(2)}) %collective-permute-start.11) | collective-permute-done | bytes 1048608 | tf_op jit(solution)/shard_map/ppermute | solution.py:13
  431.1 97.0 %fusion.215 = f32[128,1,2048]{2,1,0:T(1,128)S(1)} fusion(bf16[1,255,2048]{2,1,0:T(8,128)(2,1)S(1)} %maximum_bitcast_fusion, bf16[1,128,2048]{2,1,0:T(8,128)(2,1)} %bitcast.44), kind=kOutput, calls=%fused_computation.368 | convolution fusion | flops 67108864 | bytes 2617344 | tf_op jit(solution)/shard_map/transpose(jvp())/conv_general_dilated | solution.py:28
  530.8 12.0 %fusion.217 = f32[1,128,2048]{2,0,1:T(1,128)} fusion(f32[128,1,2048]{2,1,0:T(1,128)S(1)} %copy-done.33, bf16[1,255,2048]{2,1,0:T(8,128)(2,1)S(1)} %maximum_bitcast_fusion), kind=kOutput, calls=%fused_computation.370 | convolution fusion | flops 402653184 | bytes 3141632 | tf_op jit(solution)/shard_map/jvp()/conv_general_dilated | solution.py:28
  555.1 83.0 %all-reduce.2.cloned.1.call-done = f32[128,128]{0,1:T(8,128)} async-done(((f32[128,128]{0,1:T(8,128)}), f32[128,128]{0,1:T(8,128)}) %all-reduce.2.cloned.1.call-update) | async-done | bytes 65552 | tf_op jit(solution)/shard_map/psum | solution.py:220
  (474 shorter events, 311.3 us)
Async XLA Ops:
  7.2 354.7 %reduce-scatter.2.cloned.1.call-start = ((), (), s32[]{:S(2)}) async-start(), calls=%async_computation.1 | async-start | bytes 4718592 | tf_op jit(solution)/shard_map/reduce_scatter | solution.py:187
  9.1 2.9 collective-permute-start.6
  13.8 26.4 %collective-permute-start.7 = (bf16[4,256,512]{2,1,0:T(8,128)(2,1)S(1)}, bf16[4,256,512]{2,1,0:T(8,128)(2,1)S(1)}, u32[]{:S(2)}, u32[]{:S(2)}) collective-permute-start(bf16[4,256,512]{2,1,0:T(8,128)(2,1)S(1)} %broadcast_select_fusion.7), channel_id=1, source_target_pairs={{0,4},{2,6},{4,0},{6,2},{8,12},{10,14},{12,8},{14,10},{16,20},{18,... | collective-permute-start | bytes 3145736 | tf_op jit(solution)/shard_map/ppermute | solution.py:13
  40.9 24.9 %collective-permute-start.8 = (bf16[4,256,512]{2,1,0:T(8,128)(2,1)S(1)}, bf16[4,256,512]{2,1,0:T(8,128)(2,1)}, u32[]{:S(2)}, u32[]{:S(2)}) collective-permute-start(bf16[4,256,512]{2,1,0:T(8,128)(2,1)S(1)} %get-tuple-element.2627), channel_id=1, source_target_pairs={{0,8},{2,10},{4,12},{6,14},{8,0},{10,2},{12,4},{14,6},{16,24},{18,... | collective-permute-start | bytes 3145736 | tf_op jit(solution)/shard_map/ppermute | solution.py:13
  65.8 47.4 %collective-permute-start.9 = (bf16[4,256,512]{2,1,0:T(8,128)(2,1)}, bf16[4,256,512]{2,1,0:T(8,128)(2,1)S(1)}, u32[]{:S(2)}, u32[]{:S(2)}) collective-permute-start(bf16[4,256,512]{2,1,0:T(8,128)(2,1)} %collective-permute-done.8), channel_id=1, source_target_pairs={{0,16},{2,18},{4,20},{6,22},{8,24},{10,26},{12,28},{14,30},{16,0},... | collective-permute-start | bytes 3145736 | tf_op jit(solution)/shard_map/ppermute | solution.py:13
  83.7 554.4 %all-reduce.2.cloned.1.call-start = ((), (), s32[]{:S(2)}) async-start(), calls=%async_computation.2 | async-start | bytes 131072 | tf_op jit(solution)/shard_map/psum | solution.py:220
  120.5 26.4 %collective-permute-start = (bf16[2,512,4,128]{3,1,2,0:T(8,128)(2,1)S(1)}, bf16[2,512,4,128]{3,1,2,0:T(8,128)(2,1)S(1)}, u32[]{:S(2)}, u32[]{:S(2)}) collective-permute-start(bf16[2,512,4,128]{3,1,2,0:T(8,128)(2,1)S(1)} %copy.425), channel_id=1, source_target_pairs={{0,8},{2,10},{4,12},{6,14},{8,16},{10,18},{12,20},{14,22},{16,24},... | collective-permute-start | bytes 3145736 | tf_op jit(solution)/shard_map/while/body/eval_jaxpr/ppermute | solution.py:24
  147.0 25.5 %collective-permute-start = (bf16[2,512,4,128]{3,1,2,0:T(8,128)(2,1)S(1)}, bf16[2,512,4,128]{3,1,2,0:T(8,128)(2,1)S(1)}, u32[]{:S(2)}, u32[]{:S(2)}) collective-permute-start(bf16[2,512,4,128]{3,1,2,0:T(8,128)(2,1)S(1)} %copy.425), channel_id=1, source_target_pairs={{0,8},{2,10},{4,12},{6,14},{8,16},{10,18},{12,20},{14,22},{16,24},... | collective-permute-start | bytes 3145736 | tf_op jit(solution)/shard_map/while/body/eval_jaxpr/ppermute | solution.py:24
  172.6 24.6 %collective-permute-start = (bf16[2,512,4,128]{3,1,2,0:T(8,128)(2,1)S(1)}, bf16[2,512,4,128]{3,1,2,0:T(8,128)(2,1)S(1)}, u32[]{:S(2)}, u32[]{:S(2)}) collective-permute-start(bf16[2,512,4,128]{3,1,2,0:T(8,128)(2,1)S(1)} %copy.425), channel_id=1, source_target_pairs={{0,8},{2,10},{4,12},{6,14},{8,16},{10,18},{12,20},{14,22},{16,24},... | collective-permute-start | bytes 3145736 | tf_op jit(solution)/shard_map/while/body/eval_jaxpr/ppermute | solution.py:24
  216.8 24.0 %collective-permute-start.1 = (bf16[2,512,4,128]{3,1,2,0:T(8,128)(2,1)S(1)}, bf16[2,512,4,128]{3,1,2,0:T(8,128)(2,1)}, u32[]{:S(2)}, u32[]{:S(2)}) collective-permute-start(bf16[2,512,4,128]{3,1,2,0:T(8,128)(2,1)S(1)} %copy.487), channel_id=1, source_target_pairs={{0,8},{2,10},{4,12},{6,14},{8,16},{10,18},{12,20},{14,22},{16,24},... | collective-permute-start | bytes 3145736 | tf_op jit(solution)/shard_map/while/body/eval_jaxpr/ppermute | solution.py:24
  216.8 23.9 %collective-permute-start.2 = (f32[2,4,256]{2,1,0:T(4,128)S(1)}, f32[2,4,256]{2,1,0:T(4,128)S(1)}, u32[]{:S(2)}, u32[]{:S(2)}) collective-permute-start(f32[2,4,256]{2,1,0:T(4,128)S(1)} %copy.488), channel_id=1, source_target_pairs={{0,8},{2,10},{4,12},{6,14},{8,16},{10,18},{12,20},{14,22},{16,24},... | collective-permute-start | bytes 24584 | tf_op jit(solution)/shard_map/while/body/eval_jaxpr/ppermute | solution.py:24
  216.8 23.9 %collective-permute-start.3 = (f32[2,4,256]{2,1,0:T(4,128)S(1)}, f32[2,4,256]{2,1,0:T(4,128)S(1)}, u32[]{:S(2)}, u32[]{:S(2)}) collective-permute-start(f32[2,4,256]{2,1,0:T(4,128)S(1)} %copy.489), channel_id=1, source_target_pairs={{0,8},{2,10},{4,12},{6,14},{8,16},{10,18},{12,20},{14,22},{16,24},... | collective-permute-start | bytes 24584 | tf_op jit(solution)/shard_map/while/body/eval_jaxpr/ppermute | solution.py:24
  242.0 23.2 %collective-permute-start.1 = (bf16[2,512,4,128]{3,1,2,0:T(8,128)(2,1)S(1)}, bf16[2,512,4,128]{3,1,2,0:T(8,128)(2,1)}, u32[]{:S(2)}, u32[]{:S(2)}) collective-permute-start(bf16[2,512,4,128]{3,1,2,0:T(8,128)(2,1)S(1)} %copy.487), channel_id=1, source_target_pairs={{0,8},{2,10},{4,12},{6,14},{8,16},{10,18},{12,20},{14,22},{16,24},... | collective-permute-start | bytes 3145736 | tf_op jit(solution)/shard_map/while/body/eval_jaxpr/ppermute | solution.py:24
  242.7 22.3 %collective-permute-start.2 = (f32[2,4,256]{2,1,0:T(4,128)S(1)}, f32[2,4,256]{2,1,0:T(4,128)S(1)}, u32[]{:S(2)}, u32[]{:S(2)}) collective-permute-start(f32[2,4,256]{2,1,0:T(4,128)S(1)} %copy.488), channel_id=1, source_target_pairs={{0,8},{2,10},{4,12},{6,14},{8,16},{10,18},{12,20},{14,22},{16,24},... | collective-permute-start | bytes 24584 | tf_op jit(solution)/shard_map/while/body/eval_jaxpr/ppermute | solution.py:24
  244.0 21.1 %collective-permute-start.3 = (f32[2,4,256]{2,1,0:T(4,128)S(1)}, f32[2,4,256]{2,1,0:T(4,128)S(1)}, u32[]{:S(2)}, u32[]{:S(2)}) collective-permute-start(f32[2,4,256]{2,1,0:T(4,128)S(1)} %copy.489), channel_id=1, source_target_pairs={{0,8},{2,10},{4,12},{6,14},{8,16},{10,18},{12,20},{14,22},{16,24},... | collective-permute-start | bytes 24584 | tf_op jit(solution)/shard_map/while/body/eval_jaxpr/ppermute | solution.py:24
  266.4 22.3 %collective-permute-start.1 = (bf16[2,512,4,128]{3,1,2,0:T(8,128)(2,1)S(1)}, bf16[2,512,4,128]{3,1,2,0:T(8,128)(2,1)}, u32[]{:S(2)}, u32[]{:S(2)}) collective-permute-start(bf16[2,512,4,128]{3,1,2,0:T(8,128)(2,1)S(1)} %copy.487), channel_id=1, source_target_pairs={{0,8},{2,10},{4,12},{6,14},{8,16},{10,18},{12,20},{14,22},{16,24},... | collective-permute-start | bytes 3145736 | tf_op jit(solution)/shard_map/while/body/eval_jaxpr/ppermute | solution.py:24
  266.4 22.3 %collective-permute-start.2 = (f32[2,4,256]{2,1,0:T(4,128)S(1)}, f32[2,4,256]{2,1,0:T(4,128)S(1)}, u32[]{:S(2)}, u32[]{:S(2)}) collective-permute-start(f32[2,4,256]{2,1,0:T(4,128)S(1)} %copy.488), channel_id=1, source_target_pairs={{0,8},{2,10},{4,12},{6,14},{8,16},{10,18},{12,20},{14,22},{16,24},... | collective-permute-start | bytes 24584 | tf_op jit(solution)/shard_map/while/body/eval_jaxpr/ppermute | solution.py:24
  267.6 21.1 %collective-permute-start.3 = (f32[2,4,256]{2,1,0:T(4,128)S(1)}, f32[2,4,256]{2,1,0:T(4,128)S(1)}, u32[]{:S(2)}, u32[]{:S(2)}) collective-permute-start(f32[2,4,256]{2,1,0:T(4,128)S(1)} %copy.489), channel_id=1, source_target_pairs={{0,8},{2,10},{4,12},{6,14},{8,16},{10,18},{12,20},{14,22},{16,24},... | collective-permute-start | bytes 24584 | tf_op jit(solution)/shard_map/while/body/eval_jaxpr/ppermute | solution.py:24
  361.8 22.6 %collective-permute-start.10 = (bf16[4,256,512]{2,1,0:T(8,128)(2,1)}, bf16[4,256,512]{2,1,0:T(8,128)(2,1)}, u32[]{:S(2)}, u32[]{:S(2)}) collective-permute-start(bf16[4,256,512]{2,1,0:T(8,128)(2,1)} %slice.496), channel_id=1, source_target_pairs={{0,8},{2,10},{4,12},{6,14},{8,0},{10,2},{12,4},{14,6},{16,24},{18,... | collective-permute-start | bytes 3145736 | tf_op jit(solution)/shard_map/ppermute | solution.py:13
  363.8 23.9 %collective-permute-start.5 = (bf16[127,2048]{1,0:T(8,128)(2,1)}, bf16[127,2048]{1,0:T(8,128)(2,1)}, u32[]{:S(2)}, u32[]{:S(2)}) collective-permute-start(bf16[127,2048]{1,0:T(8,128)(2,1)} %bitcast.241), channel_id=1, source_target_pairs={{2,0},{4,2},{6,4},{8,6},{10,8},{12,10},{14,12},{16,14},{18,16},{20... | collective-permute-start | bytes 1560584 | tf_op jit(solution)/shard_map/ppermute | solution.py:19
  384.4 39.2 %collective-permute-start.11 = (bf16[4,256,512]{2,1,0:T(8,128)(2,1)}, bf16[4,256,512]{2,1,0:T(8,128)(2,1)}, u32[]{:S(2)}, u32[]{:S(2)}) collective-permute-start(bf16[4,256,512]{2,1,0:T(8,128)(2,1)} %collective-permute-done.10), channel_id=1, source_target_pairs={{0,16},{2,18},{4,20},{6,22},{8,24},{10,26},{12,28},{14,30},{16,0},... | collective-permute-start | bytes 3145736 | tf_op jit(solution)/shard_map/ppermute | solution.py:13
  403.8 26.0 %collective-permute-start.4 = (bf16[127,2048]{1,0:T(8,128)(2,1)}, bf16[127,2048]{1,0:T(8,128)(2,1)}, u32[]{:S(2)}, u32[]{:S(2)}) collective-permute-start(bf16[127,2048]{1,0:T(8,128)(2,1)} %slice_bitcast_fusion.12), channel_id=1, source_target_pairs={{0,2},{2,4},{4,6},{6,8},{8,10},{10,12},{12,14},{14,16},{16,18},{18... | collective-permute-start | bytes 1560584 | tf_op jit(solution)/shard_map/ppermute | solution.py:19
  425.8 102.2 %collective-permute-start.12 = (bf16[4,256,512]{2,1,0:T(8,128)(2,1)}, bf16[4,256,512]{2,1,0:T(8,128)(2,1)}, u32[]{:S(2)}, u32[]{:S(2)}) collective-permute-start(bf16[4,256,512]{2,1,0:T(8,128)(2,1)} %broadcast_select_fusion.3), channel_id=1, source_target_pairs={{0,4},{2,6},{4,0},{6,2},{8,12},{10,14},{12,8},{14,10},{16,20},{18,... | collective-permute-start | bytes 3145736 | tf_op jit(solution)/shard_map/ppermute | solution.py:13
  530.8 108.9 %collective-permute-start.13 = (bf16[4,128,1024]{2,1,0:T(8,128)(2,1)}, bf16[4,128,1024]{2,1,0:T(8,128)(2,1)}, u32[]{:S(2)}, u32[]{:S(2)}) collective-permute-start(bf16[4,128,1024]{2,1,0:T(8,128)(2,1)} %broadcast_select_fusion.11), channel_id=1, source_target_pairs={{0,2},{2,0},{4,6},{6,4},{8,10},{10,8},{12,14},{14,12},{16,18},{18,... | collective-permute-start | bytes 3145736 | tf_op jit(solution)/shard_map/ppermute | solution.py:13
  (51 other events, 331.3 us)
Sparse Core Ops, SparseCore 0:
  83.8 42.5 reduce-scatter.1
  551.0 87.0 all-reduce.1
where the time goes:
time: 657 us; the launch traced here: 650 us
  waiting for transfers between devices  255 us (39%)
  matrix products  214 us (33%)
  local copies, waits for them, and re-layouts  92.2 us (14%)
  other arithmetic  36.4 us (6%)
  starting transfers between devices  23.3 us (4%)
  between operations  15.1 us (2%)
  loops' own time  13.1 us (2%)
    conv_general_dilated x3, matrix products, depthwise(): lax.conv_general_dilated(padded[None], kernel[:, None, :], (1,), 'VALID',...  120 us
    ppermute x8, waiting for transfers between devices, from_partner(): lax.ppermute(shard, axis, [(i, i ^ 1 << apart) for i in range(lax.axis_si...  99.9 us
    psum x1, waiting for transfers between devices, local(): filter_grad = lax.psum(local_grad, 'ctx')  83 us
    ppermute x12, waiting for transfers between devices, from_behind(): lax.ppermute(shard, axis, [(i, (i + by) % peers) for i in range(peers)])  72.5 us
    dot_general x27, matrix products, masked_scores(): jnp.einsum('qhd,khd->hqk', query_block, key_block, preferred_element_type...  43 us
    unnamed x85, local copies, waits for them, and re-layouts  16.6 us
    ppermute x8, starting transfers between devices, from_partner(): lax.ppermute(shard, axis, [(i, i ^ 1 << apart) for i in range(lax.axis_si...  15.2 us
    dot_general x9, matrix products, query_work(): jnp.einsum('hqk,khd->hqd', dscores, key_block, preferred_element_type=jnp...  15 us
  transfers between devices with their start and end apart: 24, of which 16 were waited for; matrix products, arithmetic and copies ran while one was open for 50% of the time, Pallas kernels for 0%

commit v1 on v0

--- a/solution.py
+++ b/solution.py
@@ -1,6 +1,8 @@
 import jax
 import jax.numpy as jnp
 from jax import lax
+from jax.experimental import pallas as pl
+from jax.experimental.pallas import tpu as pltpu
 from jax.sharding import PartitionSpec as P
 
 HEAD_DIM = 128
@@ -22,19 +24,6 @@
 def from_behind(shard, axis, by):
     peers = lax.axis_size(axis)
     return lax.ppermute(shard, axis, [(i, (i + by) % peers) for i in range(peers)])
-
-
-def depthwise(padded, kernel):
-    result = lax.conv_general_dilated(
-        padded[None],
-        kernel[:, None, :],
-        (1,),
-        "VALID",
-        dimension_numbers=("NWC", "WIO", "NWC"),
-        feature_group_count=kernel.shape[1],
-        precision=lax.Precision.HIGHEST,
-    )
-    return result[0]
 
 
 def heads_in(stacked, position, bit):
@@ -174,50 +163,185 @@
     return lax.cond(key_start < query_start + query_block.shape[0], key_work, keep_state, grads)
 
 
-def local(tokens, feature_table, mr_filter, hyena_cot, queries, keys, values, attn_cot):
-    tok_rows = tokens.shape[0]
-    vocab_part = feature_table.shape[0]
-    first_id = lax.axis_index("ch") * vocab_part
-    matches = tokens[:, None] == first_id + lax.iota(jnp.int32, vocab_part)[None, :]
-    partial_rows = jnp.dot(
-        matches.astype(jnp.bfloat16),
-        feature_table.reshape(vocab_part, -1),
-        preferred_element_type=jnp.float32,
-    )
-    summed = lax.psum_scatter(
-        partial_rows.reshape(tok_rows, 3, -1).astype(jnp.bfloat16),
-        "ch",
-        scatter_dimension=2,
-        tiled=True,
-    )
-    channels = summed.shape[2]
-    gate_in = summed[:, 0].astype(jnp.float32)
-    gate_out = summed[:, 1].astype(jnp.float32)
-    value_in = summed[:, 2].astype(jnp.float32)
-    mixed = (gate_in * value_in).astype(jnp.bfloat16)
-    taps = mr_filter.shape[0]
-    reach = taps - 1
-    earlier = passed_along(mixed[tok_rows - reach :], "ctx", 1)
-    padded = jnp.concatenate([earlier, mixed], 0).astype(jnp.float32)
-    per_channel = jnp.repeat(mr_filter, channels // mr_filter.shape[1], axis=1)
-    long_conv, pullback = jax.vjp(depthwise, padded, per_channel[::-1])
-    hyena_out = (gate_out * long_conv).astype(jnp.bfloat16)
-    cotangent = hyena_cot.astype(jnp.float32)
-    conv_cot = (cotangent * gate_out).astype(jnp.bfloat16)
-    padded_grad, kernel_grad = pullback(conv_cot.astype(jnp.float32))
-    later = passed_along(conv_cot[:reach], "ctx", -1)
-    extended = jnp.concatenate([conv_cot, later], 0).astype(jnp.float32)
-    mixed_grad = depthwise(extended, per_channel)
-    feat_grads = jnp.stack(
-        [
-            (mixed_grad * value_in).astype(jnp.bfloat16),
-            (cotangent * long_conv).astype(jnp.bfloat16),
-            (mixed_grad * gate_in).astype(jnp.bfloat16),
-        ],
-        axis=1,
-    )
-    local_grad = kernel_grad[::-1].reshape(taps, mr_filter.shape[1], -1).sum(axis=2)
-    filter_grad = lax.psum(local_grad, "ctx")
+LANES = 128
+
+
+def dot(left, right, left_dim, right_dim):
+    return lax.dot_general(
+        left, right, (((left_dim,), (right_dim,)), ((), ())), preferred_element_type=jnp.float32
+    )
+
+
+def hyena_kernel(
+    per_group, mixed, earlier, conv_cot, later, gate_in, gate_out, value_in, cot,
+    back_rows, ahead_rows, hyena_out, grad_in, grad_out, grad_value, filter_part,
+):
+    rows = mixed.shape[0]
+    span = 2 * rows
+    window = jnp.concatenate([earlier[...], mixed[...]], 0)
+    cot_here = conv_cot[...]
+    ahead = jnp.concatenate([cot_here, later[...]], 0)
+    row_id = lax.broadcasted_iota(jnp.int32, (rows, rows), 0)
+    col_id = lax.broadcasted_iota(jnp.int32, (rows, rows), 1)
+    flip = (row_id + col_id == rows - 1).astype(jnp.float32).astype(jnp.bfloat16)
+    flipped = dot(flip, cot_here, 1, 0)
+    lane_group = lax.broadcasted_iota(jnp.int32, (rows, LANES), 1) // per_group
+    long_conv = jnp.zeros((rows, LANES), jnp.float32)
+    mixed_grad = jnp.zeros((rows, LANES), jnp.float32)
+
+    def toeplitz(row):
+        spread = jnp.broadcast_to(row, (rows, span))
+        return pltpu.roll(spread, 0, 1, stride=1, stride_axis=0).astype(jnp.bfloat16)
+
+    for number in range(LANES // per_group):
+        mine = lane_group == number
+        back = toeplitz(back_rows[0, number : number + 1, :])
+        long_conv = jnp.where(mine, dot(back, window, 1, 0), long_conv)
+        forward = toeplitz(ahead_rows[0, number : number + 1, :])
+        mixed_grad = jnp.where(mine, dot(forward, ahead, 1, 0), mixed_grad)
+        picked = jnp.where(mine, flipped, 0.0).astype(jnp.bfloat16)
+        products = dot(picked, window, 1, 1)
+        aligned = pltpu.roll(products, 0, 1, stride=1, stride_axis=0)
+        filter_part[0, number : number + 1, :] = jnp.sum(aligned, axis=0, keepdims=True)
+    hyena_out[...] = (gate_out[...].astype(jnp.float32) * long_conv).astype(jnp.bfloat16)
+    grad_in[...] = (mixed_grad * value_in[...].astype(jnp.float32)).astype(jnp.bfloat16)
+    grad_out[...] = (cot[...].astype(jnp.float32) * long_conv).astype(jnp.bfloat16)
+    grad_value[...] = (mixed_grad * gate_in[...].astype(jnp.float32)).astype(jnp.bfloat16)
+
+
+def hyena(mixed, earlier, conv_cot, later, gate_in, gate_out, value_in, cot, mr_filter):
+    rows, channels = mixed.shape
+    taps, groups = mr_filter.shape
+    per_group = channels // groups
+    per_step = LANES // per_group
+    steps = channels // LANES
+    span = 2 * rows
+    by_group = mr_filter.T
+    blank = jnp.zeros((groups, span - taps), jnp.float32)
+    back_rows = jnp.concatenate([blank[:, :1], by_group[:, ::-1], blank[:, 1:]], 1)
+    ahead_rows = jnp.concatenate([by_group, blank], 1)
+    block = pl.BlockSpec((rows, LANES), lambda step: (0, step))
+    per = pl.BlockSpec((1, per_step, span), lambda step: (step, 0, 0))
+
+    def body(*refs):
+        hyena_kernel(per_group, *refs)
+
+    wide = jax.ShapeDtypeStruct((rows, channels), jnp.bfloat16)
+    *outs, parts = pl.pallas_call(
+        body,
+        grid=(steps,),
+        in_specs=[block] * 8 + [per] * 2,
+        out_specs=[block] * 4 + [per],
+        out_shape=[wide] * 4 + [jax.ShapeDtypeStruct((steps, per_step, span), jnp.float32)],
+        cost_estimate=pl.CostEstimate(
+            flops=12 * rows * span * channels * per_step, bytes_accessed=12 * rows * channels * 2,
+            transcendentals=0,
+        ),
+        compiler_params=pltpu.CompilerParams(vmem_limit_bytes=32 * 1024 * 1024),
+    )(
+        mixed, earlier, conv_cot, later, gate_in, gate_out, value_in, cot,
+        back_rows.reshape(steps, per_step, span), ahead_rows.reshape(steps, per_step, span),
+    )
+    local_grad = parts.reshape(groups, span)[:, span - taps :][:, ::-1].T
+    return outs, local_grad
+
+
+def attention_kernel(block, arrays, results, keys_across, values_across, cots_across, key_sum, value_sum):
+    count, _, length, _ = arrays.shape
+    total = count * length
+    scale = HEAD_DIM ** (-0.5)
+    per = block // length
+
+    def take(which, first, last):
+        return arrays[first:last, which].reshape((last - first) * length, HEAD_DIM)
+
+    def put(which, first, last, value):
+        results[first:last, which] = value.astype(jnp.bfloat16).reshape(
+            last - first, length, HEAD_DIM
+        )
+
+    keys_across[...] = take(1, 0, count).T
+    values_across[...] = take(2, 0, count).T
+    cots_across[...] = take(3, 0, count).T
+    key_row = lax.broadcasted_iota(jnp.int32, (block, block), 0)
+    query_col = lax.broadcasted_iota(jnp.int32, (block, block), 1)
+    allowed = key_row <= query_col
+    for step in reversed(range(total // block)):
+        first, last = step * per, (step + 1) * per
+        here = slice(step * block, (step + 1) * block)
+        queries, cots = take(0, first, last), take(3, first, last)
+        pieces = []
+        for part in range(step + 1):
+            piece = dot(take(1, part * per, (part + 1) * per), queries, 1, 1) * scale
+            pieces.append(jnp.where(allowed, piece, NEG) if part == step else piece)
+        row_max = pieces[0].max(axis=0, keepdims=True)
+        for piece in pieces[1:]:
+            row_max = jnp.maximum(row_max, piece.max(axis=0, keepdims=True))
+        probs = [jnp.exp(piece - row_max) for piece in pieces]
+        row_total = probs[0].sum(axis=0, keepdims=True)
+        for piece in probs[1:]:
+            row_total = row_total + piece.sum(axis=0, keepdims=True)
+        weighted = None
+        for part, piece in enumerate(probs):
+            span = slice(part * block, (part + 1) * block)
+            term = dot(values_across[:, span], piece.astype(jnp.bfloat16), 1, 0)
+            weighted = term if weighted is None else weighted + term
+        inverse = 1.0 / row_total
+        output = (weighted * inverse).astype(jnp.bfloat16).astype(jnp.float32)
+        put(0, first, last, output.T)
+        delta = jnp.sum(cots_across[:, here].astype(jnp.float32) * output, axis=0, keepdims=True)
+        query_grad = None
+        for part, piece in enumerate(probs):
+            span = slice(part * block, (part + 1) * block)
+            piece = piece * inverse
+            value_term = dot(piece.astype(jnp.bfloat16), cots, 1, 0)
+            dprobs = dot(take(2, part * per, (part + 1) * per), cots, 1, 1)
+            dscores = (piece * (dprobs - delta)).astype(jnp.bfloat16)
+            key_term = dot(dscores, queries, 1, 0)
+            if step == total // block - 1:
+                value_sum[span], key_sum[span] = value_term, key_term
+            else:
+                value_sum[span] += value_term
+                key_sum[span] += key_term
+            term = dot(keys_across[:, span], dscores, 1, 0)
+            query_grad = term if query_grad is None else query_grad + term
+        put(1, first, last, (query_grad * scale).T)
+    put(2, 0, count, key_sum[...] * scale)
+    put(3, 0, count, value_sum[...])
+
+
+def whole_head(queries, keys, values, attn_cot):
+    peers = lax.axis_size("ctx")
+    length, width = queries.shape
+    split = [
+        array.reshape(length, peers, HEAD_DIM).transpose(1, 0, 2)
+        for array in (queries, keys, values, attn_cot)
+    ]
+    arrays = lax.all_to_all(jnp.stack(split, 1), "ctx", 0, 0)
+    total = peers * length
+    across = pltpu.VMEM((HEAD_DIM, total), jnp.bfloat16)
+    down = pltpu.VMEM((total, HEAD_DIM), jnp.float32)
+
+    def body(*refs):
+        attention_kernel(2 * length, *refs)
+
+    results = pl.pallas_call(
+        body,
+        in_specs=[pl.BlockSpec(memory_space=pltpu.VMEM)],
+        out_specs=pl.BlockSpec(memory_space=pltpu.VMEM),
+        out_shape=jax.ShapeDtypeStruct(arrays.shape, jnp.bfloat16),
+        scratch_shapes=[across] * 3 + [down] * 2,
+        cost_estimate=pl.CostEstimate(
+            flops=7 * total * total * HEAD_DIM, bytes_accessed=16 * total * HEAD_DIM,
+            transcendentals=total * total // 2,
+        ),
+        compiler_params=pltpu.CompilerParams(vmem_limit_bytes=48 * 1024 * 1024),
+    )(arrays)
+    results = lax.all_to_all(results, "ctx", 0, 0)
+    return [results[:, which].transpose(1, 0, 2).reshape(length, width) for which in range(4)]
+
+
+def ring_attention(queries, keys, values, attn_cot):
     position = lax.axis_index("ctx")
     stacked = jnp.stack([queries, keys, values, attn_cot])
     for bit in (0, 1):
@@ -363,7 +487,52 @@
     result = fold_rows(result, bits)
     for bit in (1, 0):
         result = heads_out(result, position, bit)
-    return (hyena_out, feat_grads, filter_grad, result[0], result[1], result[2], result[3])
+    return result[0], result[1], result[2], result[3]
+
+
+def summed_over(value, axis):
+    step = 1
+    while step < lax.axis_size(axis):
+        pairs = [(i, i ^ step) for i in range(lax.axis_size(axis))]
+        value = value + lax.ppermute(value, axis, pairs)
+        step *= 2
+    return value
+
+
+def looked_up(tokens, feature_table):
+    vocab_part = feature_table.shape[0]
+    first_id = lax.axis_index("ch") * vocab_part
+    matches = tokens[:, None] == first_id + lax.iota(jnp.int32, vocab_part)[None, :]
+    matches = matches.astype(jnp.bfloat16)
+    partial = jnp.einsum(
+        "tv,vic->itc", matches, feature_table, preferred_element_type=jnp.float32
+    ).astype(jnp.bfloat16)
+    peers = lax.axis_size("ch")
+    if peers != 2:
+        return lax.psum_scatter(partial, "ch", scatter_dimension=2, tiled=True)
+    width = partial.shape[2] // 2
+    upper = lax.axis_index("ch") == 1
+    low, high = partial[:, :, :width], partial[:, :, width:]
+    given = jnp.where(upper, low, high)
+    return jnp.where(upper, high, low) + lax.ppermute(given, "ch", [(0, 1), (1, 0)])
+
+
+def local(tokens, feature_table, mr_filter, hyena_cot, queries, keys, values, attn_cot):
+    gate_in, gate_out, value_in = looked_up(tokens, feature_table)
+    mixed = (gate_in.astype(jnp.float32) * value_in.astype(jnp.float32)).astype(jnp.bfloat16)
+    conv_cot = (hyena_cot.astype(jnp.float32) * gate_out.astype(jnp.float32)).astype(jnp.bfloat16)
+    earlier = passed_along(mixed, "ctx", 1)
+    later = passed_along(conv_cot, "ctx", -1)
+    outs, local_grad = hyena(
+        mixed, earlier, conv_cot, later, gate_in, gate_out, value_in, hyena_cot, mr_filter
+    )
+    feat_grads = jnp.stack(outs[1:], axis=1)
+    filter_grad = summed_over(local_grad, "ctx")
+    if queries.shape[1] == lax.axis_size("ctx") * HEAD_DIM:
+        attention = whole_head(queries, keys, values, attn_cot)
+    else:
+        attention = ring_attention(queries, keys, values, attn_cot)
+    return (outs[0], feat_grads, filter_grad, *attention)
 
 
 def solution(mesh):

time: 657 us -> 177 us (0.27); the launches traced: 650 us -> 177 us
  waiting for transfers between devices: 255 us -> 41.9 us
  matrix products: 214 us -> 3.81 us
  local copies, waits for them, and re-layouts: 92.2 us -> 16.5 us
  starting transfers between devices: 23.3 us -> 74.7 us
  Pallas kernels: 0 us -> 30.5 us
  other arithmetic: 36.4 us -> 8.23 us
  between operations: 15.1 us -> 0.98 us
  loops' own time: 13.1 us -> 0 us
    ppermute x20 -> x5, waiting for transfers between devices: 172 us -> 7.13 us  [the longest x4 7.13 us: summed_over(): value = value + lax.ppermute(value, axis, pairs)]
    conv_general_dilated x3 -> x0, matrix products: 120 us -> none  [depthwise(): lax.conv_general_dilated(padded[None], kernel[:, None, :], (1,), 'VALID',...]
    dot_general x64 -> x1, matrix products: 93.7 us -> 3.81 us  [looked_up(): jnp.einsum('tv,vic->itc', matches, feature_table, preferred_element_type=...]
    psum x1 -> x0, waiting for transfers between devices: 83 us -> none  [local(): filter_grad = lax.psum(local_grad, 'ctx')]
    all_to_all x0 -> x2, waiting for transfers between devices: none -> 33.6 us  [the longest x1 33.6 us: whole_head(): arrays = lax.all_to_all(jnp.stack(split, 1), 'ctx', 0, 0)]
    ppermute x20 -> x5, starting transfers between devices: 19.8 us -> 52.2 us  [the longest x4 50.7 us: summed_over(): value = value + lax.ppermute(value, axis, pairs)]
    pallas_call x0 -> x2, Pallas kernels: none -> 30.5 us  [the longest x1 16 us: hyena(): pl.pallas_call(body, grid=(steps,), in_specs=[block] * 8 + [per] * 2, out...]
    all_to_all x0 -> x2, starting transfers between devices: none -> 18.9 us  [the longest x1 11.4 us: whole_head(): results = lax.all_to_all(results, 'ctx', 0, 0)]
  transfers between devices with their start and end apart: 24 -> 9, of which waited for: 16 -> 6; matrix products, arithmetic and copies ran while one was open for 50% -> 7% of each run, Pallas kernels for 0% -> 17%
where the time goes in v1:
time: 177 us
  starting transfers between devices  74.7 us (42%)
  waiting for transfers between devices  41.9 us (24%)
  Pallas kernels  30.5 us (17%)
  local copies, waits for them, and re-layouts  16.5 us (9%)
  other arithmetic  8.23 us (5%)
  matrix products  3.81 us (2%)
    ppermute x4, starting transfers between devices, summed_over(): value = value + lax.ppermute(value, axis, pairs)  50.7 us
    all_to_all x1, waiting for transfers between devices, whole_head(): arrays = lax.all_to_all(jnp.stack(split, 1), 'ctx', 0, 0)  33.6 us
    pallas_call x1, Pallas kernels, hyena(): pl.pallas_call(body, grid=(steps,), in_specs=[block] * 8 + [per] * 2, out...  16 us
    pallas_call x1, Pallas kernels, whole_head(): pl.pallas_call(body, in_specs=[pl.BlockSpec(memory_space=pltpu.VMEM)], ou...  14.5 us
    all_to_all x1, starting transfers between devices, whole_head(): results = lax.all_to_all(results, 'ctx', 0, 0)  11.4 us
    unnamed x34, local copies, waits for them, and re-layouts  10.8 us
    all_to_all x1, starting transfers between devices, whole_head(): arrays = lax.all_to_all(jnp.stack(split, 1), 'ctx', 0, 0)  7.52 us
    ppermute x4, waiting for transfers between devices, summed_over(): value = value + lax.ppermute(value, axis, pairs)  7.13 us
  transfers between devices with their start and end apart: 9, of which 6 were waited for; matrix products, arithmetic and copies ran while one was open for 7% of the time, Pallas kernels for 17%

profile of v1, /device:TPU:0, one launch (start us, length us, event | category | flops | bytes accessed | tf_op | source)
XLA Modules:
  0.0 176.6 jit_solution(8387459825042421827)
XLA Ops:
  0.7 1.4 copy.21
  4.1 1.6 pad_maximum_fusion
  5.7 7.5 %all-to-all-start = ((bf16[16,4,128,128]{3,2,1,0:T(8,128)(2,1)}), bf16[16,4,128,128]{3,2,1,0:T(8,128)(2,1)S(1)}, u32[]{:S(2)}, u32[]{:S(2)}) async-start(bf16[16,4,128,128]{3,2,1,0:T(8,128)(2,1)} %pad_maximum_fusion), calls=%async_computation | async-start | bytes 4194304 | tf_op jit(solution)/shard_map/all_to_all | solution.py:320
  13.3 3.8 %fusion = bf16[3,128,4096]{2,1,0:T(8,128)(2,1)S(1)} fusion(bf16[256,3,4096]{2,0,1:T(8,128)(2,1)} %param.9, s32[256]{0:T(256)S(1)} %iota_add_fusion, s32[128]{0:T(128)S(1)} %copy-done.11), kind=kOutput, calls=%fused_computation.1 | convolution fusion | flops 806912000 | bytes 9438720 | tf_op jit(solution)/shard_map/tv,vic->itc/dot_general | solution.py:507
  17.1 1.5 broadcast_select_fusion
  19.2 1.5 collective-permute-start
  20.7 33.6 %all-to-all-done.refs_0_ = bf16[16,4,128,128]{3,2,1,0:T(8,128)(2,1)S(1)} async-done(((bf16[16,4,128,128]{3,2,1,0:T(8,128)(2,1)}), bf16[16,4,128,128]{3,2,1,0:T(8,128)(2,1)S(1)}, u32[]{:S(2)}, u32[]{:S(2)}) %all-to-all-start) | async-done | bytes 2097184 | tf_op jit(solution)/shard_map/all_to_all | solution.py:320
  54.4 14.5 %shard_map.136 = bf16[16,4,128,128]{3,2,1,0:T(8,128)(2,1)} custom-call(bf16[16,4,128,128]{3,2,1,0:T(8,128)(2,1)S(1)} %all-to-all-done.refs_0_), custom_call_target="tpu_custom_call" | custom-call | flops 3758096384 | bytes 4194304 | tf_op jit(solution)/shard_map/pallas_call | solution.py:328
  68.9 11.4 %all-to-all-start.1 = ((bf16[16,4,128,128]{3,2,1,0:T(8,128)(2,1)}), bf16[16,4,128,128]{3,2,1,0:T(8,128)(2,1)}, u32[]{:S(2)}, u32[]{:S(2)}) async-start(bf16[16,4,128,128]{3,2,1,0:T(8,128)(2,1)} %shard_map.136), calls=%async_computation.1 | async-start | bytes 4194304 | tf_op jit(solution)/shard_map/all_to_all | solution.py:340
  80.7 2.6 %select_add_fusion = bf16[3,128,2048]{2,1,0:T(8,128)(2,1)S(1)} fusion(bf16[3,128,2048]{2,1,0:T(8,128)(2,1)} %collective-permute-done, pred[]{:T(512)S(6)} %eq.16, bf16[3,128,4096]{2,1,0:T(8,128)(2,1)} %copy-done.5), kind=kLoop, calls=%fused_computation.4 | loop fusion | flops 1572864 | bytes 6291457 | tf_op jit(solution)/shard_map/add | solution.py:517
  83.7 2.3 %collective-permute-start.1 = (bf16[128,2048]{1,0:T(8,128)(2,1)S(1)}, bf16[128,2048]{1,0:T(8,128)(2,1)S(1)}, u32[]{:S(2)}, u32[]{:S(2)}) collective-permute-start(bf16[128,2048]{1,0:T(8,128)(2,1)S(1)} %get-tuple-element.32.refs_0_), channel_id=1, source_target_pairs={{0,2},{2,4},{4,6},{6,8},{8,10},{10,12},{12,14},{14,16},{16,18},{18... | collective-permute-start | bytes 1572872 | tf_op jit(solution)/shard_map/ppermute | solution.py:21
  86.0 1.3 collective-permute-start.2
  87.5 1.5 slice_bitcast_fusion.5
  89.8 1.1 collective-permute-done.2.refs_3_
  93.8 16.0 %shard_map.135 = (bf16[128,2048]{1,0:T(8,128)(2,1)}, bf16[128,2048]{1,0:T(8,128)(2,1)S(1)}, bf16[128,2048]{1,0:T(8,128)(2,1)S(1)}, bf16[128,2048]{1,0:T(8,128)(2,1)S(1)}, f32[16,8,256]{2,1,0:T(8,128)S(1)}) custom-call(bf16[128,2048]{1,0:T(8,128)(2,1)S(1)} %get-tuple-element.32.refs_0_, bf16[128,2048]{1,0:T(8,128)(2,1)S(1)} %copy-done.2, ...), custom_call_target="tpu_custom_call" | custom-call | flops 6442450944 | bytes 6291456 | tf_op jit(solution)/shard_map/pallas_call | solution.py:230
  109.9 14.4 %collective-permute-start.3 = (f32[128,128]{1,0:T(8,128)S(1)}, f32[128,128]{1,0:T(8,128)S(1)}, u32[]{:S(2)}, u32[]{:S(2)}) collective-permute-start(f32[128,128]{1,0:T(8,128)S(1)} %bitcast.82), channel_id=1, source_target_pairs={{0,2},{2,0},{4,6},{6,4},{8,10},{10,8},{12,14},{14,12},{16,18},{18,... | collective-permute-start | bytes 196616 | tf_op jit(solution)/shard_map/ppermute | solution.py:497
  125.2 18.6 %collective-permute-start.4 = (f32[128,128]{1,0:T(8,128)S(1)}, f32[128,128]{1,0:T(8,128)S(1)}, u32[]{:S(2)}, u32[]{:S(2)}) collective-permute-start(f32[128,128]{1,0:T(8,128)S(1)} %bitcast_add_fusion), channel_id=1, source_target_pairs={{0,4},{2,6},{4,0},{6,2},{8,12},{10,14},{12,8},{14,10},{16,20},{18,... | collective-permute-start | bytes 196616 | tf_op jit(solution)/shard_map/ppermute | solution.py:497
  143.8 2.6 %collective-permute-done.4 = f32[128,128]{1,0:T(8,128)S(1)} collective-permute-done((f32[128,128]{1,0:T(8,128)S(1)}, f32[128,128]{1,0:T(8,128)S(1)}, u32[]{:S(2)}, u32[]{:S(2)}) %collective-permute-start.4) | collective-permute-done | bytes 65568 | tf_op jit(solution)/shard_map/ppermute | solution.py:497
  146.5 13.0 %collective-permute-start.5 = (f32[128,128]{1,0:T(8,128)S(1)}, f32[128,128]{1,0:T(8,128)S(1)}, u32[]{:S(2)}, u32[]{:S(2)}) collective-permute-start(f32[128,128]{1,0:T(8,128)S(1)} %add.32), channel_id=1, source_target_pairs={{0,8},{2,10},{4,12},{6,14},{8,0},{10,2},{12,4},{14,6},{16,24},{18,... | collective-permute-start | bytes 196616 | tf_op jit(solution)/shard_map/ppermute | solution.py:497
  159.5 2.2 %collective-permute-done.5 = f32[128,128]{1,0:T(8,128)S(1)} collective-permute-done((f32[128,128]{1,0:T(8,128)S(1)}, f32[128,128]{1,0:T(8,128)S(1)}, u32[]{:S(2)}, u32[]{:S(2)}) %collective-permute-start.5) | collective-permute-done | bytes 65568 | tf_op jit(solution)/shard_map/ppermute | solution.py:497
  161.7 4.7 %collective-permute-start.6 = (f32[128,128]{1,0:T(8,128)S(1)}, f32[128,128]{1,0:T(8,128)S(1)}, u32[]{:S(2)}, u32[]{:S(2)}) collective-permute-start(f32[128,128]{1,0:T(8,128)S(1)} %add.33), channel_id=1, source_target_pairs={{0,16},{2,18},{4,20},{6,22},{8,24},{10,26},{12,28},{14,30},{16,0},... | collective-permute-start | bytes 196616 | tf_op jit(solution)/shard_map/ppermute | solution.py:497
  166.4 1.3 pad_maximum_fusion.1
  167.8 1.4 collective-permute-done.6
  169.8 1.7 slice_bitcast_fusion
  (60 shorter events, 14.0 us)
Async XLA Ops:
  0.6 1.7 copy-start.7
  0.6 2.3 %copy-start.8 = (bf16[128,2048]{1,0:T(8,128)(2,1)S(1)}, bf16[128,2048]{1,0:T(8,128)(2,1)}, u32[]{:S(2)}) copy-start(bf16[128,2048]{1,0:T(8,128)(2,1)} %param.14) | copy-start | bytes 1572868
  2.4 1.2 copy-start.9
  5.7 7.5 %copy-start.11 = (s32[128]{0:T(128)S(1)}, s32[128]{0:T(128)}, u32[]{:S(2)}) copy-start(s32[128]{0:T(128)} %param.8) | copy-start | bytes 1540
  5.7 48.6 %all-to-all-start = ((bf16[16,4,128,128]{3,2,1,0:T(8,128)(2,1)}), bf16[16,4,128,128]{3,2,1,0:T(8,128)(2,1)S(1)}, u32[]{:S(2)}, u32[]{:S(2)}) async-start(bf16[16,4,128,128]{3,2,1,0:T(8,128)(2,1)} %pad_maximum_fusion), calls=%async_computation | async-start | bytes 4194304 | tf_op jit(solution)/shard_map/all_to_all | solution.py:320
  17.1 2.1 %copy-start.5 = (bf16[3,128,4096]{2,1,0:T(8,128)(2,1)}, bf16[3,128,4096]{2,1,0:T(8,128)(2,1)S(1)}, u32[]{:S(2)}) copy-start(bf16[3,128,4096]{2,1,0:T(8,128)(2,1)S(1)} %fusion) | copy-start | bytes 9437188
  19.2 61.4 %collective-permute-start = (bf16[3,128,2048]{2,1,0:T(8,128)(2,1)}, bf16[3,128,2048]{2,1,0:T(8,128)(2,1)}, u32[]{:S(2)}, u32[]{:S(2)}) collective-permute-start(bf16[3,128,2048]{2,1,0:T(8,128)(2,1)} %broadcast_select_fusion), channel_id=1, source_target_pairs={{0,1},{1,0},{2,3},{3,2},{4,5},{5,4},{6,7},{7,6},{8,9},{9,8},{10,11... | collective-permute-start | bytes 4718600 | tf_op jit(solution)/shard_map/ppermute | solution.py:517
  68.9 11.4 %copy-start.10 = (f32[128,128]{1,0:T(8,128)S(1)}, f32[128,128]{1,0:T(8,128)}, u32[]{:S(2)}) copy-start(f32[128,128]{1,0:T(8,128)} %param.10) | copy-start | bytes 196612
  68.9 100.9 %all-to-all-start.1 = ((bf16[16,4,128,128]{3,2,1,0:T(8,128)(2,1)}), bf16[16,4,128,128]{3,2,1,0:T(8,128)(2,1)}, u32[]{:S(2)}, u32[]{:S(2)}) async-start(bf16[16,4,128,128]{3,2,1,0:T(8,128)(2,1)} %shard_map.136), calls=%async_computation.1 | async-start | bytes 4194304 | tf_op jit(solution)/shard_map/all_to_all | solution.py:340
  80.6 2.7 %copy-start = (bf16[128,2048]{1,0:T(8,128)(2,1)S(1)}, bf16[128,2048]{1,0:T(8,128)(2,1)}, u32[]{:S(2)}) copy-start(bf16[128,2048]{1,0:T(8,128)(2,1)} %refs_7_.1) | copy-start | bytes 1572868
  83.3 4.0 %copy-start.6 = (bf16[3,128,2048]{2,1,0:T(8,128)(2,1)}, bf16[3,128,2048]{2,1,0:T(8,128)(2,1)S(1)}, u32[]{:S(2)}) copy-start(bf16[3,128,2048]{2,1,0:T(8,128)(2,1)S(1)} %select_add_fusion) | copy-start | bytes 4718596
  83.7 5.3 %collective-permute-start.1 = (bf16[128,2048]{1,0:T(8,128)(2,1)S(1)}, bf16[128,2048]{1,0:T(8,128)(2,1)S(1)}, u32[]{:S(2)}, u32[]{:S(2)}) collective-permute-start(bf16[128,2048]{1,0:T(8,128)(2,1)S(1)} %get-tuple-element.32.refs_0_), channel_id=1, source_target_pairs={{0,2},{2,4},{4,6},{6,8},{8,10},{10,12},{12,14},{14,16},{16,18},{18... | collective-permute-start | bytes 1572872 | tf_op jit(solution)/shard_map/ppermute | solution.py:21
  86.0 4.9 %collective-permute-start.2 = (bf16[128,2048]{1,0:T(8,128)(2,1)S(1)}, bf16[128,2048]{1,0:T(8,128)(2,1)S(1)}, u32[]{:S(2)}, u32[]{:S(2)}) collective-permute-start(bf16[128,2048]{1,0:T(8,128)(2,1)S(1)} %get-tuple-element.31.refs_2_), channel_id=1, source_target_pairs={{2,0},{4,2},{6,4},{8,6},{10,8},{12,10},{14,12},{16,14},{18,16},{20... | collective-permute-start | bytes 1572872 | tf_op jit(solution)/shard_map/ppermute | solution.py:21
  89.0 0.8 copy-start.1
  90.9 0.8 copy-start.3
  91.7 1.0 copy-start.2
  92.8 1.0 copy-start.4
  109.9 15.3 %collective-permute-start.3 = (f32[128,128]{1,0:T(8,128)S(1)}, f32[128,128]{1,0:T(8,128)S(1)}, u32[]{:S(2)}, u32[]{:S(2)}) collective-permute-start(f32[128,128]{1,0:T(8,128)S(1)} %bitcast.82), channel_id=1, source_target_pairs={{0,2},{2,0},{4,6},{6,4},{8,10},{10,8},{12,14},{14,12},{16,18},{18,... | collective-permute-start | bytes 196616 | tf_op jit(solution)/shard_map/ppermute | solution.py:497
  125.2 21.2 %collective-permute-start.4 = (f32[128,128]{1,0:T(8,128)S(1)}, f32[128,128]{1,0:T(8,128)S(1)}, u32[]{:S(2)}, u32[]{:S(2)}) collective-permute-start(f32[128,128]{1,0:T(8,128)S(1)} %bitcast_add_fusion), channel_id=1, source_target_pairs={{0,4},{2,6},{4,0},{6,2},{8,12},{10,14},{12,8},{14,10},{16,20},{18,... | collective-permute-start | bytes 196616 | tf_op jit(solution)/shard_map/ppermute | solution.py:497
  146.5 15.3 %collective-permute-start.5 = (f32[128,128]{1,0:T(8,128)S(1)}, f32[128,128]{1,0:T(8,128)S(1)}, u32[]{:S(2)}, u32[]{:S(2)}) collective-permute-start(f32[128,128]{1,0:T(8,128)S(1)} %add.32), channel_id=1, source_target_pairs={{0,8},{2,10},{4,12},{6,14},{8,0},{10,2},{12,4},{14,6},{16,24},{18,... | collective-permute-start | bytes 196616 | tf_op jit(solution)/shard_map/ppermute | solution.py:497
  161.7 7.4 %collective-permute-start.6 = (f32[128,128]{1,0:T(8,128)S(1)}, f32[128,128]{1,0:T(8,128)S(1)}, u32[]{:S(2)}, u32[]{:S(2)}) collective-permute-start(f32[128,128]{1,0:T(8,128)S(1)} %add.33), channel_id=1, source_target_pairs={{0,16},{2,18},{4,20},{6,22},{8,24},{10,26},{12,28},{14,30},{16,0},... | collective-permute-start | bytes 196616 | tf_op jit(solution)/shard_map/ppermute | solution.py:497

commit v2 on v1

--- a/solution.py
+++ b/solution.py
@@ -310,14 +310,48 @@
     put(3, 0, count, value_sum[...])
 
 
-def whole_head(queries, keys, values, attn_cot):
+def pack_kernel(*refs):
+    *sources, packed = refs
+    for which, source in enumerate(sources):
+        for head in range(packed.shape[0]):
+            packed[head, which] = source[:, head * HEAD_DIM : (head + 1) * HEAD_DIM]
+
+
+def unpack_kernel(packed, *targets):
+    for which, target in enumerate(targets):
+        for head in range(packed.shape[0]):
+            target[:, head * HEAD_DIM : (head + 1) * HEAD_DIM] = packed[head, which]
+
+
+def repacked(kernel, arrays, out_shape, length, heads, packed_in):
+    per = max(1, heads // 4)
+    flat = pl.BlockSpec((length, per * HEAD_DIM), lambda step: (0, step))
+    packed = pl.BlockSpec((per, 4, length, HEAD_DIM), lambda step: (step, 0, 0, 0))
+    return pl.pallas_call(
+        kernel,
+        grid=(heads // per,),
+        in_specs=[packed] if packed_in else [flat] * 4,
+        out_specs=[flat] * 4 if packed_in else packed,
+        out_shape=out_shape,
+        cost_estimate=pl.CostEstimate(
+            flops=0, bytes_accessed=16 * length * heads * HEAD_DIM, transcendentals=0
+        ),
+        compiler_params=pltpu.CompilerParams(vmem_limit_bytes=32 * 1024 * 1024),
+    )(*arrays)
+
+
+def heads_sent(queries, keys, values, attn_cot):
     peers = lax.axis_size("ctx")
-    length, width = queries.shape
-    split = [
-        array.reshape(length, peers, HEAD_DIM).transpose(1, 0, 2)
-        for array in (queries, keys, values, attn_cot)
-    ]
-    arrays = lax.all_to_all(jnp.stack(split, 1), "ctx", 0, 0)
+    length = queries.shape[0]
+    shape = jax.ShapeDtypeStruct((peers, 4, length, HEAD_DIM), jnp.bfloat16)
+    packed = repacked(
+        pack_kernel, (queries, keys, values, attn_cot), shape, length, peers, False
+    )
+    return lax.all_to_all(packed, "ctx", 0, 0)
+
+
+def whole_head(arrays):
+    peers, _, length, _ = arrays.shape
     total = peers * length
     across = pltpu.VMEM((HEAD_DIM, total), jnp.bfloat16)
     down = pltpu.VMEM((total, HEAD_DIM), jnp.float32)
@@ -325,7 +359,7 @@
     def body(*refs):
         attention_kernel(2 * length, *refs)
 
-    results = pl.pallas_call(
+    return pl.pallas_call(
         body,
         in_specs=[pl.BlockSpec(memory_space=pltpu.VMEM)],
         out_specs=pl.BlockSpec(memory_space=pltpu.VMEM),
@@ -337,8 +371,13 @@
         ),
         compiler_params=pltpu.CompilerParams(vmem_limit_bytes=48 * 1024 * 1024),
     )(arrays)
+
+
+def heads_back(results):
+    peers, _, length, _ = results.shape
     results = lax.all_to_all(results, "ctx", 0, 0)
-    return [results[:, which].transpose(1, 0, 2).reshape(length, width) for which in range(4)]
+    shape = [jax.ShapeDtypeStruct((length, peers * HEAD_DIM), jnp.bfloat16)] * 4
+    return repacked(unpack_kernel, (results,), shape, length, peers, True)
 
 
 def ring_attention(queries, keys, values, attn_cot):
@@ -499,26 +538,20 @@
     return value
 
 
-def looked_up(tokens, feature_table):
+def partial_rows(tokens, feature_table):
     vocab_part = feature_table.shape[0]
     first_id = lax.axis_index("ch") * vocab_part
     matches = tokens[:, None] == first_id + lax.iota(jnp.int32, vocab_part)[None, :]
-    matches = matches.astype(jnp.bfloat16)
-    partial = jnp.einsum(
-        "tv,vic->itc", matches, feature_table, preferred_element_type=jnp.float32
+    return jnp.einsum(
+        "tv,vic->itc",
+        matches.astype(jnp.bfloat16),
+        feature_table,
+        preferred_element_type=jnp.float32,
     ).astype(jnp.bfloat16)
-    peers = lax.axis_size("ch")
-    if peers != 2:
-        return lax.psum_scatter(partial, "ch", scatter_dimension=2, tiled=True)
-    width = partial.shape[2] // 2
-    upper = lax.axis_index("ch") == 1
-    low, high = partial[:, :, :width], partial[:, :, width:]
-    given = jnp.where(upper, low, high)
-    return jnp.where(upper, high, low) + lax.ppermute(given, "ch", [(0, 1), (1, 0)])
-
-
-def local(tokens, feature_table, mr_filter, hyena_cot, queries, keys, values, attn_cot):
-    gate_in, gate_out, value_in = looked_up(tokens, feature_table)
+
+
+def hyena_layer(gates, hyena_cot, mr_filter):
+    gate_in, gate_out, value_in = gates
     mixed = (gate_in.astype(jnp.float32) * value_in.astype(jnp.float32)).astype(jnp.bfloat16)
     conv_cot = (hyena_cot.astype(jnp.float32) * gate_out.astype(jnp.float32)).astype(jnp.bfloat16)
     earlier = passed_along(mixed, "ctx", 1)
@@ -526,13 +559,30 @@
     outs, local_grad = hyena(
         mixed, earlier, conv_cot, later, gate_in, gate_out, value_in, hyena_cot, mr_filter
     )
-    feat_grads = jnp.stack(outs[1:], axis=1)
+    return outs[0], jnp.stack(outs[1:], axis=1), local_grad
+
+
+def local(tokens, feature_table, mr_filter, hyena_cot, queries, keys, values, attn_cot):
+    partial = partial_rows(tokens, feature_table)
+    rows = (queries, keys, values, attn_cot)
+    if lax.axis_size("ch") != 2 or queries.shape[1] != lax.axis_size("ctx") * HEAD_DIM:
+        gates = lax.psum_scatter(partial, "ch", scatter_dimension=2, tiled=True)
+        hyena_out, feat_grads, local_grad = hyena_layer(gates, hyena_cot, mr_filter)
+        return (hyena_out, feat_grads, summed_over(local_grad, "ctx"), *ring_attention(*rows))
+    width = partial.shape[2] // 2
+    upper = lax.axis_index("ch") == 1
+    low, high = partial[:, :, :width], partial[:, :, width:]
+    given = jnp.where(upper, low, high)
+    given, rows = lax.optimization_barrier((given, rows))
+    received = lax.ppermute(given, "ch", [(0, 1), (1, 0)])
+    arrays = heads_sent(*rows)
+    gates = jnp.where(upper, high, low) + received
+    hyena_out, feat_grads, local_grad = hyena_layer(gates, hyena_cot, mr_filter)
+    arrays, local_grad = lax.optimization_barrier((arrays, local_grad))
     filter_grad = summed_over(local_grad, "ctx")
-    if queries.shape[1] == lax.axis_size("ctx") * HEAD_DIM:
-        attention = whole_head(queries, keys, values, attn_cot)
-    else:
-        attention = ring_attention(queries, keys, values, attn_cot)
-    return (outs[0], feat_grads, filter_grad, *attention)
+    results = whole_head(arrays)
+    results, filter_grad = lax.optimization_barrier((results, filter_grad))
+    return (hyena_out, feat_grads, filter_grad, *heads_back(results))
 
 
 def solution(mesh):

time: 177 us -> 177 us (level)
  the two profiles are of different devices: /device:TPU:0 before, /device:TPU:13 now
where the time goes in v2:
time: 177 us; the launch traced here: 176 us
  waiting for transfers between devices  94.6 us (53%)
  Pallas kernels  33.2 us (19%)
  starting transfers between devices  27 us (15%)
  other arithmetic  8.35 us (5%)
  local copies, waits for them, and re-layouts  8.31 us (5%)
  matrix products  3.83 us (2%)
    all_to_all x1, waiting for transfers between devices, heads_back(): results = lax.all_to_all(results, 'ctx', 0, 0)  45.1 us
    ppermute x1, waiting for transfers between devices, local(): received = lax.ppermute(given, 'ch', [(0, 1), (1, 0)])  34.4 us
    pallas_call x1, Pallas kernels, hyena(): pl.pallas_call(body, grid=(steps,), in_specs=[block] * 8 + [per] * 2, out...  16.1 us
    pallas_call x1, Pallas kernels, whole_head(): pl.pallas_call(body, in_specs=[pl.BlockSpec(memory_space=pltpu.VMEM)], ou...  13 us
    all_to_all x1, starting transfers between devices, heads_back(): results = lax.all_to_all(results, 'ctx', 0, 0)  8.82 us
    ppermute x2, waiting for transfers between devices, passed_along(): lax.ppermute(value, axis, [(source, source + steps) for source in range(l...  8.01 us
    ppermute x4, waiting for transfers between devices, summed_over(): value = value + lax.ppermute(value, axis, pairs)  7.11 us
    all_to_all x1, starting transfers between devices, heads_sent(): return lax.all_to_all(packed, 'ctx', 0, 0)  6.69 us
  transfers between devices with their start and end apart: 9, of which 7 were waited for; matrix products, arithmetic and copies ran while one was open for 5% of the time, Pallas kernels for 17%

profile of v2, /device:TPU:13, one launch (start us, length us, event | category | flops | bytes accessed | tf_op | source)
XLA Modules:
  0.0 176.1 jit_solution(8527843690394249203)
XLA Ops:
  0.6 3.8 %fusion = bf16[3,128,4096]{2,1,0:T(8,128)(2,1)S(1)} fusion(bf16[256,3,4096]{2,0,1:T(8,128)(2,1)} %param.9, s32[256]{0:T(256)S(1)} %iota_add_fusion, s32[128]{0:T(128)} %param.8), kind=kOutput, calls=%fused_computation.1 | convolution fusion | flops 806912000 | bytes 9438720 | tf_op jit(solution)/shard_map/tv,vic->itc/dot_general | solution.py:545
  4.5 1.6 copy-done.11
  6.1 1.3 broadcast_select_fusion
  8.2 2.1 %shard_map.136 = bf16[16,4,128,128]{3,2,1,0:T(8,128)(2,1)} custom-call(bf16[128,2048]{1,0:T(8,128)(2,1)S(1)} %copy-done.7, bf16[128,2048]{1,0:T(8,128)(2,1)S(1)} %copy-done.8, bf16[128,2048]{1,0:T(8,128)(2,1)S(1)} %copy-done.9, bf16[128,2048]{1,0:T(8,128)(2,1)S(1)} %copy-done.10), custom_call_target="tpu_custom_call" | custom-call | bytes 4194304 | tf_op jit(solution)/shard_map/pallas_call | solution.py:330
  10.3 6.7 %all-to-all-start = ((bf16[16,4,128,128]{3,2,1,0:T(8,128)(2,1)}), bf16[16,4,128,128]{3,2,1,0:T(8,128)(2,1)S(1)}, u32[]{:S(2)}, u32[]{:S(2)}) async-start(bf16[16,4,128,128]{3,2,1,0:T(8,128)(2,1)} %shard_map.136), calls=%async_computation | async-start | bytes 4194304 | tf_op jit(solution)/shard_map/all_to_all | solution.py:350
  17.0 1.2 collective-permute-start
  18.6 34.4 %collective-permute-done = bf16[3,128,2048]{2,1,0:T(8,128)(2,1)} collective-permute-done((bf16[3,128,2048]{2,1,0:T(8,128)(2,1)}, bf16[3,128,2048]{2,1,0:T(8,128)(2,1)}, u32[]{:S(2)}, u32[]{:S(2)}) %collective-permute-start) | collective-permute-done | bytes 1572896 | tf_op jit(solution)/shard_map/ppermute | solution.py:577
  53.0 2.6 %select_add_fusion = bf16[3,128,2048]{2,1,0:T(8,128)(2,1)S(1)} fusion(bf16[3,128,2048]{2,1,0:T(8,128)(2,1)} %collective-permute-done, pred[]{:T(512)S(6)} %eq.16, bf16[3,128,4096]{2,1,0:T(8,128)(2,1)} %copy-done.11), kind=kLoop, calls=%fused_computation.3 | loop fusion | flops 1572864 | bytes 6291457 | tf_op jit(solution)/shard_map/add | solution.py:579
  55.6 1.3 multiply_convert_fusion
  56.9 4.2 %collective-permute-start.1 = (bf16[128,2048]{1,0:T(8,128)(2,1)}, bf16[128,2048]{1,0:T(8,128)(2,1)}, u32[]{:S(2)}, u32[]{:S(2)}) collective-permute-start(bf16[128,2048]{1,0:T(8,128)(2,1)} %get-tuple-element.47.refs_0_), channel_id=1, source_target_pairs={{0,2},{2,4},{4,6},{6,8},{8,10},{10,12},{12,14},{14,16},{16,18},{18... | collective-permute-start | bytes 1572872 | tf_op jit(solution)/shard_map/ppermute | solution.py:21
  61.1 1.9 %collective-permute-start.2 = (bf16[128,2048]{1,0:T(8,128)(2,1)S(1)}, bf16[128,2048]{1,0:T(8,128)(2,1)}, u32[]{:S(2)}, u32[]{:S(2)}) collective-permute-start(bf16[128,2048]{1,0:T(8,128)(2,1)S(1)} %get-tuple-element.46.refs_2_), channel_id=1, source_target_pairs={{2,0},{4,2},{6,4},{8,6},{10,8},{12,10},{14,12},{16,14},{18,16},{20... | collective-permute-start | bytes 1572872 | tf_op jit(solution)/shard_map/ppermute | solution.py:21
  63.1 1.5 slice_bitcast_fusion.1
  64.6 3.9 %collective-permute-done.1.refs_1_ = bf16[128,2048]{1,0:T(8,128)(2,1)} collective-permute-done((bf16[128,2048]{1,0:T(8,128)(2,1)}, bf16[128,2048]{1,0:T(8,128)(2,1)}, u32[]{:S(2)}, u32[]{:S(2)}) %collective-permute-start.1) | collective-permute-done | bytes 524320 | tf_op jit(solution)/shard_map/ppermute | solution.py:21
  68.5 4.2 %collective-permute-done.2.refs_3_ = bf16[128,2048]{1,0:T(8,128)(2,1)} collective-permute-done((bf16[128,2048]{1,0:T(8,128)(2,1)S(1)}, bf16[128,2048]{1,0:T(8,128)(2,1)}, u32[]{:S(2)}, u32[]{:S(2)}) %collective-permute-start.2) | collective-permute-done | bytes 524320 | tf_op jit(solution)/shard_map/ppermute | solution.py:21
  73.7 16.1 %shard_map.135 = (bf16[128,2048]{1,0:T(8,128)(2,1)}, bf16[128,2048]{1,0:T(8,128)(2,1)S(1)}, bf16[128,2048]{1,0:T(8,128)(2,1)S(1)}, bf16[128,2048]{1,0:T(8,128)(2,1)S(1)}, f32[16,8,256]{2,1,0:T(8,128)S(1)}) custom-call(bf16[128,2048]{1,0:T(8,128)(2,1)} %get-tuple-element.47.refs_0_, bf16[128,2048]{1,0:T(8,128)(2,1)} %collective-permute-done.1.refs_1_, ...), custom_call_target="tpu_custom_call" | custom-call | flops 6442450944 | bytes 6291456 | tf_op jit(solution)/shard_map/pallas_call | solution.py:230
  91.5 3.8 %collective-permute-start.3 = (f32[128,128]{1,0:T(8,128)S(1)}, f32[128,128]{1,0:T(8,128)S(1)}, u32[]{:S(2)}, u32[]{:S(2)}) collective-permute-start(f32[128,128]{1,0:T(8,128)S(1)} %bitcast.33), channel_id=1, source_target_pairs={{0,2},{2,0},{4,6},{6,4},{8,10},{10,8},{12,14},{14,12},{16,18},{18,... | collective-permute-start | bytes 196616 | tf_op jit(solution)/shard_map/ppermute | solution.py:536
  96.3 3.1 %collective-permute-done.4 = f32[128,128]{1,0:T(8,128)S(1)} collective-permute-done((f32[128,128]{1,0:T(8,128)S(1)}, f32[128,128]{1,0:T(8,128)S(1)}, u32[]{:S(2)}, u32[]{:S(2)}) %collective-permute-start.4) | collective-permute-done | bytes 65568 | tf_op jit(solution)/shard_map/ppermute | solution.py:536
  99.5 3.1 %collective-permute-done.5 = f32[128,128]{1,0:T(8,128)S(1)} collective-permute-done((f32[128,128]{1,0:T(8,128)S(1)}, f32[128,128]{1,0:T(8,128)S(1)}, u32[]{:S(2)}, u32[]{:S(2)}) %collective-permute-start.5) | collective-permute-done | bytes 65568 | tf_op jit(solution)/shard_map/ppermute | solution.py:536
  102.9 13.0 %shard_map.137 = bf16[16,4,128,128]{3,2,1,0:T(8,128)(2,1)S(1)} custom-call(bf16[16,4,128,128]{3,2,1,0:T(8,128)(2,1)S(1)} %all-to-all-done.refs_0_), custom_call_target="tpu_custom_call" | custom-call | flops 3758096384 | bytes 4194304 | tf_op jit(solution)/shard_map/pallas_call | solution.py:362
  115.9 1.3 copy-done
  117.9 8.8 %all-to-all-start.1 = ((bf16[16,4,128,128]{3,2,1,0:T(8,128)(2,1)}), bf16[16,4,128,128]{3,2,1,0:T(8,128)(2,1)S(1)}, u32[]{:S(2)}, u32[]{:S(2)}) async-start(bf16[16,4,128,128]{3,2,1,0:T(8,128)(2,1)} %copy-done), calls=%async_computation.1 | async-start | bytes 4194304 | tf_op jit(solution)/shard_map/all_to_all | solution.py:378
  126.7 2.4 %pad_maximum_fusion = bf16[128,3,2048]{2,0,1:T(8,128)(2,1)} fusion(bf16[128,1,2048]{2,0,1:T(8,128)(2,1)} %bitcast.30, bf16[128,1,2048]{2,0,1:T(8,128)(2,1)S(1)} %bitcast.29, bf16[128,1,2048]{2,0,1:T(8,128)(2,1)S(1)} %bitcast.28), kind=kLoop, calls=%fused_computation.2 | loop fusion | flops 1572864 | bytes 3145728 | tf_op jit(solution)/shard_map/stack | solution.py:562
  129.1 45.1 %all-to-all-done.1.packed = bf16[16,4,128,128]{3,2,1,0:T(8,128)(2,1)S(1)} async-done(((bf16[16,4,128,128]{3,2,1,0:T(8,128)(2,1)}), bf16[16,4,128,128]{3,2,1,0:T(8,128)(2,1)S(1)}, u32[]{:S(2)}, u32[]{:S(2)}) %all-to-all-start.1) | async-done | bytes 2097184 | tf_op jit(solution)/shard_map/all_to_all | solution.py:378
  174.2 1.9 %shard_map.138 = (bf16[128,2048]{1,0:T(8,128)(2,1)}, bf16[128,2048]{1,0:T(8,128)(2,1)}, bf16[128,2048]{1,0:T(8,128)(2,1)}, bf16[128,2048]{1,0:T(8,128)(2,1)}) custom-call(bf16[16,4,128,128]{3,2,1,0:T(8,128)(2,1)S(1)} %all-to-all-done.1.packed), custom_call_target="tpu_custom_call" | custom-call | bytes 4194304 | tf_op jit(solution)/shard_map/pallas_call | solution.py:330
  (48 shorter events, 5.9 us)
Async XLA Ops:
  4.5 1.6 copy-start.11
  6.1 1.3 copy-start.7
  6.1 1.5 copy-start.8
  6.1 1.9 %copy-start.9 = (bf16[128,2048]{1,0:T(8,128)(2,1)S(1)}, bf16[128,2048]{1,0:T(8,128)(2,1)}, u32[]{:S(2)}) copy-start(bf16[128,2048]{1,0:T(8,128)(2,1)} %refs_2_) | copy-start | bytes 1572868
  6.1 2.1 %copy-start.10 = (bf16[128,2048]{1,0:T(8,128)(2,1)S(1)}, bf16[128,2048]{1,0:T(8,128)(2,1)}, u32[]{:S(2)}) copy-start(bf16[128,2048]{1,0:T(8,128)(2,1)} %refs_3_) | copy-start | bytes 1572868
  10.3 7.9 %copy-start.13 = (f32[128,128]{1,0:T(8,128)S(1)}, f32[128,128]{1,0:T(8,128)}, u32[]{:S(2)}) copy-start(f32[128,128]{1,0:T(8,128)} %param.10) | copy-start | bytes 196612
  10.3 81.1 %all-to-all-start = ((bf16[16,4,128,128]{3,2,1,0:T(8,128)(2,1)}), bf16[16,4,128,128]{3,2,1,0:T(8,128)(2,1)S(1)}, u32[]{:S(2)}, u32[]{:S(2)}) async-start(bf16[16,4,128,128]{3,2,1,0:T(8,128)(2,1)} %shard_map.136), calls=%async_computation | async-start | bytes 4194304 | tf_op jit(solution)/shard_map/all_to_all | solution.py:350
  17.0 35.9 %collective-permute-start = (bf16[3,128,2048]{2,1,0:T(8,128)(2,1)}, bf16[3,128,2048]{2,1,0:T(8,128)(2,1)}, u32[]{:S(2)}, u32[]{:S(2)}) collective-permute-start(bf16[3,128,2048]{2,1,0:T(8,128)(2,1)} %broadcast_select_fusion), channel_id=1, source_target_pairs={{0,1},{1,0},{2,3},{3,2},{4,5},{5,4},{6,7},{7,6},{8,9},{9,8},{10,11... | collective-permute-start | bytes 4718600 | tf_op jit(solution)/shard_map/ppermute | solution.py:577
  18.6 37.0 %copy-start.1 = (bf16[128,2048]{1,0:T(8,128)(2,1)S(1)}, bf16[128,2048]{1,0:T(8,128)(2,1)}, u32[]{:S(2)}) copy-start(bf16[128,2048]{1,0:T(8,128)(2,1)} %refs_7_.1) | copy-start | bytes 1572868
  55.6 1.3 copy-start.12
  56.9 7.8 %copy-start.5 = (bf16[128,2048]{1,0:T(8,128)(2,1)}, bf16[128,2048]{1,0:T(8,128)(2,1)S(1)}, u32[]{:S(2)}) copy-start(bf16[128,2048]{1,0:T(8,128)(2,1)S(1)} %get-tuple-element.46.refs_2_) | copy-start | bytes 1572868
  56.9 11.6 %collective-permute-start.1 = (bf16[128,2048]{1,0:T(8,128)(2,1)}, bf16[128,2048]{1,0:T(8,128)(2,1)}, u32[]{:S(2)}, u32[]{:S(2)}) collective-permute-start(bf16[128,2048]{1,0:T(8,128)(2,1)} %get-tuple-element.47.refs_0_), channel_id=1, source_target_pairs={{0,2},{2,4},{4,6},{6,8},{8,10},{10,12},{12,14},{14,16},{16,18},{18... | collective-permute-start | bytes 1572872 | tf_op jit(solution)/shard_map/ppermute | solution.py:21
  61.1 11.6 %collective-permute-start.2 = (bf16[128,2048]{1,0:T(8,128)(2,1)S(1)}, bf16[128,2048]{1,0:T(8,128)(2,1)}, u32[]{:S(2)}, u32[]{:S(2)}) collective-permute-start(bf16[128,2048]{1,0:T(8,128)(2,1)S(1)} %get-tuple-element.46.refs_2_), channel_id=1, source_target_pairs={{2,0},{4,2},{6,4},{8,6},{10,8},{12,10},{14,12},{16,14},{18,16},{20... | collective-permute-start | bytes 1572872 | tf_op jit(solution)/shard_map/ppermute | solution.py:21
  72.7 1.0 copy-start.6
  89.8 0.8 copy-start.2
  90.6 0.8 copy-start.4
  91.5 4.7 %collective-permute-start.3 = (f32[128,128]{1,0:T(8,128)S(1)}, f32[128,128]{1,0:T(8,128)S(1)}, u32[]{:S(2)}, u32[]{:S(2)}) collective-permute-start(f32[128,128]{1,0:T(8,128)S(1)} %bitcast.33), channel_id=1, source_target_pairs={{0,2},{2,0},{4,6},{6,4},{8,10},{10,8},{12,14},{14,12},{16,18},{18,... | collective-permute-start | bytes 196616 | tf_op jit(solution)/shard_map/ppermute | solution.py:536
  96.2 3.2 %collective-permute-start.4 = (f32[128,128]{1,0:T(8,128)S(1)}, f32[128,128]{1,0:T(8,128)S(1)}, u32[]{:S(2)}, u32[]{:S(2)}) collective-permute-start(f32[128,128]{1,0:T(8,128)S(1)} %add.31), channel_id=1, source_target_pairs={{0,4},{2,6},{4,0},{6,2},{8,12},{10,14},{12,8},{14,10},{16,20},{18,... | collective-permute-start | bytes 196616 | tf_op jit(solution)/shard_map/ppermute | solution.py:536
  99.4 3.2 %collective-permute-start.5 = (f32[128,128]{1,0:T(8,128)S(1)}, f32[128,128]{1,0:T(8,128)S(1)}, u32[]{:S(2)}, u32[]{:S(2)}) collective-permute-start(f32[128,128]{1,0:T(8,128)S(1)} %add.32), channel_id=1, source_target_pairs={{0,8},{2,10},{4,12},{6,14},{8,0},{10,2},{12,4},{14,6},{16,24},{18,... | collective-permute-start | bytes 196616 | tf_op jit(solution)/shard_map/ppermute | solution.py:536
  102.6 14.7 %collective-permute-start.6 = (f32[128,128]{1,0:T(8,128)S(1)}, f32[128,128]{1,0:T(8,128)S(1)}, u32[]{:S(2)}, u32[]{:S(2)}) collective-permute-start(f32[128,128]{1,0:T(8,128)S(1)} %add.33), channel_id=1, source_target_pairs={{0,16},{2,18},{4,20},{6,22},{8,24},{10,26},{12,28},{14,30},{16,0},... | collective-permute-start | bytes 196616 | tf_op jit(solution)/shard_map/ppermute | solution.py:536
  115.9 1.3 copy-start
  117.9 8.8 %copy-start.3 = (bf16[128,2048]{1,0:T(8,128)(2,1)S(1)}, bf16[128,2048]{1,0:T(8,128)(2,1)}, u32[]{:S(2)}) copy-start(bf16[128,2048]{1,0:T(8,128)(2,1)} %copy-done.2) | copy-start | bytes 1572868
  117.9 56.2 %all-to-all-start.1 = ((bf16[16,4,128,128]{3,2,1,0:T(8,128)(2,1)}), bf16[16,4,128,128]{3,2,1,0:T(8,128)(2,1)S(1)}, u32[]{:S(2)}, u32[]{:S(2)}) async-start(bf16[16,4,128,128]{3,2,1,0:T(8,128)(2,1)} %copy-done), calls=%async_computation.1 | async-start | bytes 4194304 | tf_op jit(solution)/shard_map/all_to_all | solution.py:378

commit v3 on v2

--- a/solution.py
+++ b/solution.py
@@ -375,7 +375,6 @@
 
 def heads_back(results):
     peers, _, length, _ = results.shape
-    results = lax.all_to_all(results, "ctx", 0, 0)
     shape = [jax.ShapeDtypeStruct((length, peers * HEAD_DIM), jnp.bfloat16)] * 4
     return repacked(unpack_kernel, (results,), shape, length, peers, True)
 
@@ -575,14 +574,14 @@
     given = jnp.where(upper, low, high)
     given, rows = lax.optimization_barrier((given, rows))
     received = lax.ppermute(given, "ch", [(0, 1), (1, 0)])
-    arrays = heads_sent(*rows)
+    results = whole_head(heads_sent(*rows))
+    returned = lax.all_to_all(results, "ctx", 0, 0)
+    received, _ = lax.optimization_barrier((received, results))
     gates = jnp.where(upper, high, low) + received
     hyena_out, feat_grads, local_grad = hyena_layer(gates, hyena_cot, mr_filter)
-    arrays, local_grad = lax.optimization_barrier((arrays, local_grad))
+    local_grad, _ = lax.optimization_barrier((local_grad, returned))
     filter_grad = summed_over(local_grad, "ctx")
-    results = whole_head(arrays)
-    results, filter_grad = lax.optimization_barrier((results, filter_grad))
-    return (hyena_out, feat_grads, filter_grad, *heads_back(results))
+    return (hyena_out, feat_grads, filter_grad, *heads_back(returned))
 
 
 def solution(mesh):

time: 177 us -> 179 us (1.011)
  the two profiles are of different devices: /device:TPU:13 before, /device:TPU:0 now
where the time goes in v3:
time: 179 us; the launch traced here: 178 us
  blocking collectives  54.5 us (30%)
  waiting for transfers between devices  42.6 us (24%)
  Pallas kernels  31.6 us (18%)
  starting transfers between devices  28.1 us (16%)
  other arithmetic  8.51 us (5%)
  local copies, waits for them, and re-layouts  8.34 us (5%)
  matrix products  3.83 us (2%)
    all_to_all x1, blocking collectives, heads_sent(): return lax.all_to_all(packed, 'ctx', 0, 0)  54.5 us
    ppermute x1, waiting for transfers between devices, local(): received = lax.ppermute(given, 'ch', [(0, 1), (1, 0)])  35.1 us
    ppermute x4, starting transfers between devices, summed_over(): value = value + lax.ppermute(value, axis, pairs)  17.8 us
    pallas_call x1, Pallas kernels, hyena(): pl.pallas_call(body, grid=(steps,), in_specs=[block] * 8 + [per] * 2, out...  16.1 us
    pallas_call x1, Pallas kernels, whole_head(): pl.pallas_call(body, in_specs=[pl.BlockSpec(memory_space=pltpu.VMEM)], ou...  13 us
    unnamed x28, local copies, waits for them, and re-layouts  6.59 us
    ppermute x4, waiting for transfers between devices, summed_over(): value = value + lax.ppermute(value, axis, pairs)  5.56 us
    all_to_all x1, starting transfers between devices, local(): returned = lax.all_to_all(results, 'ctx', 0, 0)  5.24 us
  transfers between devices with their start and end apart: 8, of which 5 were waited for; matrix products, arithmetic and copies ran while one was open for 5% of the time, Pallas kernels for 10%

profile of v3, /device:TPU:0, one launch (start us, length us, event | category | flops | bytes accessed | tf_op | source)
XLA Modules:
  0.0 178.3 jit_solution(145697190978689438)
XLA Ops:
  0.6 3.8 %fusion = bf16[3,128,4096]{2,1,0:T(8,128)(2,1)S(1)} fusion(bf16[256,3,4096]{2,0,1:T(8,128)(2,1)} %param.9, s32[256]{0:T(256)S(1)} %iota_add_fusion, s32[128]{0:T(128)} %param.8), kind=kOutput, calls=%fused_computation.1 | convolution fusion | flops 806912000 | bytes 9438720 | tf_op jit(solution)/shard_map/tv,vic->itc/dot_general | solution.py:544
  4.5 1.6 copy-done.10
  6.1 1.3 broadcast_select_fusion
  8.8 54.5 %all_to_all.10.refs_0_ = bf16[16,4,128,128]{3,2,1,0:T(8,128)(2,1)S(1)} all-to-all(bf16[16,4,128,128]{3,2,1,0:T(8,128)(2,1)S(1)} %shard_map.135), channel_id=1, replica_groups=mesh['ctx'=16,'ch'=2] {'ctx'}, dimensions={0} | all-to-all | bytes 4194304 | tf_op jit(solution)/shard_map/all_to_all | solution.py:350
  63.3 13.0 %shard_map.136 = bf16[16,4,128,128]{3,2,1,0:T(8,128)(2,1)S(1)} custom-call(bf16[16,4,128,128]{3,2,1,0:T(8,128)(2,1)S(1)} %all_to_all.10.refs_0_), custom_call_target="tpu_custom_call" | custom-call | flops 3758096384 | bytes 4194304 | tf_op jit(solution)/shard_map/pallas_call | solution.py:362
  76.4 1.4 copy-done
  77.7 5.2 %all-to-all-start.1 = ((bf16[16,4,128,128]{3,2,1,0:T(8,128)(2,1)}), bf16[16,4,128,128]{3,2,1,0:T(8,128)(2,1)S(1)}, u32[]{:S(2)}, u32[]{:S(2)}) async-start(bf16[16,4,128,128]{3,2,1,0:T(8,128)(2,1)} %copy-done), calls=%async_computation.1 | async-start | bytes 4194304 | tf_op jit(solution)/shard_map/all_to_all | solution.py:578
  83.0 1.6 collective-permute-start
  84.9 35.1 %collective-permute-done = bf16[3,128,2048]{2,1,0:T(8,128)(2,1)} collective-permute-done((bf16[3,128,2048]{2,1,0:T(8,128)(2,1)}, bf16[3,128,2048]{2,1,0:T(8,128)(2,1)}, u32[]{:S(2)}, u32[]{:S(2)}) %collective-permute-start) | collective-permute-done | bytes 1572896 | tf_op jit(solution)/shard_map/ppermute | solution.py:576
  120.0 2.6 %select_add_fusion = bf16[3,128,2048]{2,1,0:T(8,128)(2,1)S(1)} fusion(bf16[3,128,2048]{2,1,0:T(8,128)(2,1)} %collective-permute-done, pred[]{:T(512)S(6)} %eq.16, bf16[3,128,4096]{2,1,0:T(8,128)(2,1)} %copy-done.10), kind=kLoop, calls=%fused_computation.3 | loop fusion | flops 1572864 | bytes 6291457 | tf_op jit(solution)/shard_map/add | solution.py:580
  122.6 1.3 multiply_convert_fusion
  123.9 2.3 %collective-permute-start.1 = (bf16[128,2048]{1,0:T(8,128)(2,1)}, bf16[128,2048]{1,0:T(8,128)(2,1)}, u32[]{:S(2)}, u32[]{:S(2)}) collective-permute-start(bf16[128,2048]{1,0:T(8,128)(2,1)} %get-tuple-element.43.refs_0_), channel_id=1, source_target_pairs={{0,2},{2,4},{4,6},{6,8},{8,10},{10,12},{12,14},{14,16},{16,18},{18... | collective-permute-start | bytes 1572872 | tf_op jit(solution)/shard_map/ppermute | solution.py:21
  126.2 1.3 collective-permute-start.2
  127.6 1.5 slice_bitcast_fusion.1
  129.2 1.9 %collective-permute-done.2.refs_3_ = bf16[128,2048]{1,0:T(8,128)(2,1)} collective-permute-done((bf16[128,2048]{1,0:T(8,128)(2,1)S(1)}, bf16[128,2048]{1,0:T(8,128)(2,1)}, u32[]{:S(2)}, u32[]{:S(2)}) %collective-permute-start.2) | collective-permute-done | bytes 524320 | tf_op jit(solution)/shard_map/ppermute | solution.py:21
  132.1 16.1 %shard_map.137 = (bf16[128,2048]{1,0:T(8,128)(2,1)}, bf16[128,2048]{1,0:T(8,128)(2,1)S(1)}, bf16[128,2048]{1,0:T(8,128)(2,1)S(1)}, bf16[128,2048]{1,0:T(8,128)(2,1)S(1)}, f32[16,8,256]{2,1,0:T(8,128)S(1)}) custom-call(bf16[128,2048]{1,0:T(8,128)(2,1)} %get-tuple-element.43.refs_0_, bf16[128,2048]{1,0:T(8,128)(2,1)} %collective-permute-done.1.refs_1_, ...), custom_call_target="tpu_custom_call" | custom-call | flops 6442450944 | bytes 6291456 | tf_op jit(solution)/shard_map/pallas_call | solution.py:230
  149.9 8.7 %collective-permute-start.3 = (f32[128,128]{1,0:T(8,128)S(1)}, f32[128,128]{1,0:T(8,128)S(1)}, u32[]{:S(2)}, u32[]{:S(2)}) collective-permute-start(f32[128,128]{1,0:T(8,128)S(1)} %bitcast.33), channel_id=1, source_target_pairs={{0,2},{2,0},{4,6},{6,4},{8,10},{10,8},{12,14},{14,12},{16,18},{18,... | collective-permute-start | bytes 196616 | tf_op jit(solution)/shard_map/ppermute | solution.py:535
  159.5 2.8 %collective-permute-start.4 = (f32[128,128]{1,0:T(8,128)S(1)}, f32[128,128]{1,0:T(8,128)S(1)}, u32[]{:S(2)}, u32[]{:S(2)}) collective-permute-start(f32[128,128]{1,0:T(8,128)S(1)} %add.31), channel_id=1, source_target_pairs={{0,4},{2,6},{4,0},{6,2},{8,12},{10,14},{12,8},{14,10},{16,20},{18,... | collective-permute-start | bytes 196616 | tf_op jit(solution)/shard_map/ppermute | solution.py:535
  162.2 2.4 %collective-permute-done.4 = f32[128,128]{1,0:T(8,128)S(1)} collective-permute-done((f32[128,128]{1,0:T(8,128)S(1)}, f32[128,128]{1,0:T(8,128)S(1)}, u32[]{:S(2)}, u32[]{:S(2)}) %collective-permute-start.4) | collective-permute-done | bytes 65568 | tf_op jit(solution)/shard_map/ppermute | solution.py:535
  164.7 3.5 %collective-permute-start.5 = (f32[128,128]{1,0:T(8,128)S(1)}, f32[128,128]{1,0:T(8,128)S(1)}, u32[]{:S(2)}, u32[]{:S(2)}) collective-permute-start(f32[128,128]{1,0:T(8,128)S(1)} %add.32), channel_id=1, source_target_pairs={{0,8},{2,10},{4,12},{6,14},{8,0},{10,2},{12,4},{14,6},{16,24},{18,... | collective-permute-start | bytes 196616 | tf_op jit(solution)/shard_map/ppermute | solution.py:535
  168.1 2.2 %collective-permute-done.5 = f32[128,128]{1,0:T(8,128)S(1)} collective-permute-done((f32[128,128]{1,0:T(8,128)S(1)}, f32[128,128]{1,0:T(8,128)S(1)}, u32[]{:S(2)}, u32[]{:S(2)}) %collective-permute-start.5) | collective-permute-done | bytes 65568 | tf_op jit(solution)/shard_map/ppermute | solution.py:535
  170.4 2.9 %collective-permute-start.6 = (f32[128,128]{1,0:T(8,128)S(1)}, f32[128,128]{1,0:T(8,128)S(1)}, u32[]{:S(2)}, u32[]{:S(2)}) collective-permute-start(f32[128,128]{1,0:T(8,128)S(1)} %add.33), channel_id=1, source_target_pairs={{0,16},{2,18},{4,20},{6,22},{8,24},{10,26},{12,28},{14,30},{16,0},... | collective-permute-start | bytes 196616 | tf_op jit(solution)/shard_map/ppermute | solution.py:535
  173.3 2.5 %pad_maximum_fusion = bf16[128,3,2048]{2,0,1:T(8,128)(2,1)} fusion(bf16[128,1,2048]{2,0,1:T(8,128)(2,1)} %bitcast.30, bf16[128,1,2048]{2,0,1:T(8,128)(2,1)} %bitcast.29, bf16[128,1,2048]{2,0,1:T(8,128)(2,1)S(1)} %bitcast.28), kind=kLoop, calls=%fused_computation.2 | loop fusion | flops 1572864 | bytes 3145728 | tf_op jit(solution)/shard_map/stack | solution.py:561
  175.8 1.9 %shard_map.138 = (bf16[128,2048]{1,0:T(8,128)(2,1)}, bf16[128,2048]{1,0:T(8,128)(2,1)}, bf16[128,2048]{1,0:T(8,128)(2,1)}, bf16[128,2048]{1,0:T(8,128)(2,1)}) custom-call(bf16[16,4,128,128]{3,2,1,0:T(8,128)(2,1)S(1)} %all-to-all-done.1.packed), custom_call_target="tpu_custom_call" | custom-call | bytes 4194304 | tf_op jit(solution)/shard_map/pallas_call | solution.py:330
  (45 shorter events, 6.1 us)
Async XLA Ops:
  4.5 1.6 copy-start.10
  6.1 1.3 copy-start.6
  6.1 1.5 copy-start.7
  6.1 1.9 %copy-start.8 = (bf16[128,2048]{1,0:T(8,128)(2,1)S(1)}, bf16[128,2048]{1,0:T(8,128)(2,1)}, u32[]{:S(2)}) copy-start(bf16[128,2048]{1,0:T(8,128)(2,1)} %refs_2_) | copy-start | bytes 1572868
  6.1 2.1 %copy-start.9 = (bf16[128,2048]{1,0:T(8,128)(2,1)S(1)}, bf16[128,2048]{1,0:T(8,128)(2,1)}, u32[]{:S(2)}) copy-start(bf16[128,2048]{1,0:T(8,128)(2,1)} %refs_3_) | copy-start | bytes 1572868
  76.4 1.4 copy-start
  77.7 6.8 %copy-start.12 = (f32[128,128]{1,0:T(8,128)S(1)}, f32[128,128]{1,0:T(8,128)}, u32[]{:S(2)}) copy-start(f32[128,128]{1,0:T(8,128)} %param.10) | copy-start | bytes 196612
  77.7 72.1 %all-to-all-start.1 = ((bf16[16,4,128,128]{3,2,1,0:T(8,128)(2,1)}), bf16[16,4,128,128]{3,2,1,0:T(8,128)(2,1)S(1)}, u32[]{:S(2)}, u32[]{:S(2)}) async-start(bf16[16,4,128,128]{3,2,1,0:T(8,128)(2,1)} %copy-done), calls=%async_computation.1 | async-start | bytes 4194304 | tf_op jit(solution)/shard_map/all_to_all | solution.py:578
  83.0 37.0 %collective-permute-start = (bf16[3,128,2048]{2,1,0:T(8,128)(2,1)}, bf16[3,128,2048]{2,1,0:T(8,128)(2,1)}, u32[]{:S(2)}, u32[]{:S(2)}) collective-permute-start(bf16[3,128,2048]{2,1,0:T(8,128)(2,1)} %broadcast_select_fusion), channel_id=1, source_target_pairs={{0,1},{1,0},{2,3},{3,2},{4,5},{5,4},{6,7},{7,6},{8,9},{9,8},{10,11... | collective-permute-start | bytes 4718600 | tf_op jit(solution)/shard_map/ppermute | solution.py:576
  84.9 37.7 %copy-start.1 = (bf16[128,2048]{1,0:T(8,128)(2,1)S(1)}, bf16[128,2048]{1,0:T(8,128)(2,1)}, u32[]{:S(2)}) copy-start(bf16[128,2048]{1,0:T(8,128)(2,1)} %refs_7_.1) | copy-start | bytes 1572868
  122.6 1.3 copy-start.11
  123.9 5.2 %copy-start.4 = (bf16[128,2048]{1,0:T(8,128)(2,1)}, bf16[128,2048]{1,0:T(8,128)(2,1)S(1)}, u32[]{:S(2)}) copy-start(bf16[128,2048]{1,0:T(8,128)(2,1)S(1)} %get-tuple-element.42.refs_2_) | copy-start | bytes 1572868
  123.9 5.2 %collective-permute-start.1 = (bf16[128,2048]{1,0:T(8,128)(2,1)}, bf16[128,2048]{1,0:T(8,128)(2,1)}, u32[]{:S(2)}, u32[]{:S(2)}) collective-permute-start(bf16[128,2048]{1,0:T(8,128)(2,1)} %get-tuple-element.43.refs_0_), channel_id=1, source_target_pairs={{0,2},{2,4},{4,6},{6,8},{8,10},{10,12},{12,14},{14,16},{16,18},{18... | collective-permute-start | bytes 1572872 | tf_op jit(solution)/shard_map/ppermute | solution.py:21
  126.2 4.9 %collective-permute-start.2 = (bf16[128,2048]{1,0:T(8,128)(2,1)S(1)}, bf16[128,2048]{1,0:T(8,128)(2,1)}, u32[]{:S(2)}, u32[]{:S(2)}) collective-permute-start(bf16[128,2048]{1,0:T(8,128)(2,1)S(1)} %get-tuple-element.42.refs_2_), channel_id=1, source_target_pairs={{2,0},{4,2},{6,4},{8,6},{10,8},{12,10},{14,12},{16,14},{18,16},{20... | collective-permute-start | bytes 1572872 | tf_op jit(solution)/shard_map/ppermute | solution.py:21
  131.1 1.0 copy-start.5
  148.2 0.8 copy-start.2
  149.0 0.8 copy-start.3
  149.9 9.6 %collective-permute-start.3 = (f32[128,128]{1,0:T(8,128)S(1)}, f32[128,128]{1,0:T(8,128)S(1)}, u32[]{:S(2)}, u32[]{:S(2)}) collective-permute-start(f32[128,128]{1,0:T(8,128)S(1)} %bitcast.33), channel_id=1, source_target_pairs={{0,2},{2,0},{4,6},{6,4},{8,10},{10,8},{12,14},{14,12},{16,18},{18,... | collective-permute-start | bytes 196616 | tf_op jit(solution)/shard_map/ppermute | solution.py:535
  159.5 5.2 %collective-permute-start.4 = (f32[128,128]{1,0:T(8,128)S(1)}, f32[128,128]{1,0:T(8,128)S(1)}, u32[]{:S(2)}, u32[]{:S(2)}) collective-permute-start(f32[128,128]{1,0:T(8,128)S(1)} %add.31), channel_id=1, source_target_pairs={{0,4},{2,6},{4,0},{6,2},{8,12},{10,14},{12,8},{14,10},{16,20},{18,... | collective-permute-start | bytes 196616 | tf_op jit(solution)/shard_map/ppermute | solution.py:535
  164.7 5.7 %collective-permute-start.5 = (f32[128,128]{1,0:T(8,128)S(1)}, f32[128,128]{1,0:T(8,128)S(1)}, u32[]{:S(2)}, u32[]{:S(2)}) collective-permute-start(f32[128,128]{1,0:T(8,128)S(1)} %add.32), channel_id=1, source_target_pairs={{0,8},{2,10},{4,12},{6,14},{8,0},{10,2},{12,4},{14,6},{16,24},{18,... | collective-permute-start | bytes 196616 | tf_op jit(solution)/shard_map/ppermute | solution.py:535
  170.4 7.3 %collective-permute-start.6 = (f32[128,128]{1,0:T(8,128)S(1)}, f32[128,128]{1,0:T(8,128)S(1)}, u32[]{:S(2)}, u32[]{:S(2)}) collective-permute-start(f32[128,128]{1,0:T(8,128)S(1)} %add.33), channel_id=1, source_target_pairs={{0,16},{2,18},{4,20},{6,22},{8,24},{10,26},{12,28},{14,30},{16,0},... | collective-permute-start | bytes 196616 | tf_op jit(solution)/shard_map/ppermute | solution.py:535
